TPU v7x, 128 devices: a whole 4x4x4 slice. The times are simulated.
128 devices in a mesh: chan: 64 (over x, z_hi, y, core), win: 2 (over z_lo).
Axes of the slice: x: 4, y: 4, z: 4 (z_hi: 2, z_lo: 2; z = z_hi * 2 + z_lo), core: 2. Of those that a mesh axis runs over, the one named last changes fastest.
Arguments:
- spectra: bfloat16 [2, 256, 64, 8192], P(None, None, 'win', 'chan'), may hold values from -6 to 6
- freq_idx: int32 [64], replicated, may hold values from 0 to 255
- pairing: int32 [6, 64], replicated, may hold values from 0 to 63, as said below
Outputs:
- crossspec: bfloat16 [2, 6, 64, 8192, 128], P(None, None, 'win', 'chan')
Inputs may be any that keep to these rules, and one draw needn't show every extreme that they name: Each row pairs the 64 blocks two by two: pairing[r, pairing[r, b]] = b and pairing[r, b] != b.
All inputs are finite; a program needn't handle non-finite values.
Results may differ from a plain program's by a relative error of at most 0.012.
Values may be sent and summed in bfloat16 or wider, within the bound.
A program may use at most 192 MiB of HBM per device.

v0:
```python
import math

import jax
import jax.numpy as jnp
from jax import lax
from jax.sharding import PartitionSpec as P


def pair_products(left, right):
    return jnp.einsum("fwbi,fwbj->fbij", left, right, preferred_element_type=jnp.float32)


def body(spectra, freq_idx, pairing):
    nblocks = lax.axis_size("chan")
    selected = jnp.take(spectra, freq_idx, axis=1)
    gathered = lax.all_to_all(selected, "chan", split_axis=1, concat_axis=3, tiled=True)
    fbins = gathered.shape[1]
    width = gathered.shape[2]
    block_size = spectra.shape[3]
    blocks = gathered.reshape(2, fbins, width, nblocks, block_size)
    scale = 1.0 / math.sqrt(width * lax.axis_size("win"))
    results = []
    for step in range(pairing.shape[0]):
        partner = jnp.take(blocks, pairing[step], axis=3)
        real_part = pair_products(blocks[0], partner[0]) + pair_products(blocks[1], partner[1])
        imag_part = pair_products(blocks[1], partner[0]) - pair_products(blocks[0], partner[1])
        results.append(jnp.stack([real_part, imag_part]) * scale)
    partial_value = jnp.stack(results, 1).reshape(
        2, pairing.shape[0], fbins, nblocks * block_size, block_size
    )
    partial_value = lax.optimization_barrier(partial_value.astype(jnp.bfloat16))
    moved = lax.all_to_all(partial_value, "chan", split_axis=3, concat_axis=2, tiled=True)
    return lax.psum_scatter(
        moved.astype(jnp.float32).astype(jnp.bfloat16), "win", scatter_dimension=2, tiled=True
    )


def solution(mesh):
    return jax.shard_map(
        body,
        mesh=mesh,
        in_specs=(P(None, None, "win", "chan"), P(), P()),
        out_specs=P(None, None, "win", "chan", None),
        check_vma=False,
    )
```

profile of v0, /device:TPU:1, one launch (start us, length us, event | category | flops | bytes accessed | tf_op | source)
XLA Modules:
  0.0 803.2 jit_solution(8622064597698110577)
XLA Ops:
  7.9 2.9 gather_fusion
  12.0 12.3 %all-to-all-start = ((bf16[2,64,32,128]{3,2,0,1:T(8,128)(2,1)}), bf16[2,64,32,128]{3,2,0,1:T(8,128)(2,1)S(1)}, u32[]{:S(2)}, u32[]{:S(2)}) async-start(bf16[2,64,32,128]{3,2,0,1:T(8,128)(2,1)} %select_bitcast_fusion), calls=%async_computation | async-start | bytes 2097152 | tf_op jit(solution)/shard_map/all_to_all | solution.py:16
  24.4 19.3 %all-to-all-done = bf16[2,64,32,128]{3,2,0,1:T(8,128)(2,1)S(1)} async-done(((bf16[2,64,32,128]{3,2,0,1:T(8,128)(2,1)}), bf16[2,64,32,128]{3,2,0,1:T(8,128)(2,1)S(1)}, u32[]{:S(2)}, u32[]{:S(2)}) %all-to-all-start) | async-done | bytes 1048608 | tf_op jit(solution)/shard_map/all_to_all | solution.py:16
  44.7 2.7 fusion.7
  47.4 2.8 fusion.6
  53.3 2.8 fusion.9
  56.1 2.8 fusion.8
  61.9 2.7 fusion.11
  64.6 2.7 fusion.10
  70.4 2.8 fusion.13
  73.2 2.8 fusion.12
  76.0 1.7 gather_fusion.5
  79.1 2.8 fusion.15
  81.9 2.7 fusion.14
  87.7 2.7 fusion.17
  90.5 2.8 fusion.16
  110.4 2.9 convolution_add_fusion.1
  113.3 5.0 convolution_subtract_fusion.1
  118.3 4.9 convolution_add_fusion
  123.2 5.0 convolution_subtract_fusion
  128.2 9.1 %bitcast_dynamic-update-slice_fusion.4 = bf16[2,6,1,8192,128]{4,0,2,1,3:T(2,128)(2,1)} fusion(f32[1,1,8192,128]{3,0,2,1:T(1,128)S(1)} %bitcast.240, f32[1,1,8192,128]{3,0,2,1:T(1,128)S(1)} %bitcast.239), kind=kLoop, calls=%fused_computation.24 | loop fusion | flops 6291455 | bytes 12582912
  137.3 9.1 %bitcast_dynamic-update-slice_fusion.3 = bf16[2,6,1,8192,128]{4,0,2,1,3:T(2,128)(2,1)} fusion(bf16[2,6,1,8192,128]{4,0,2,1,3:T(2,128)(2,1)} %bitcast_dynamic-update-slice_fusion.4, f32[1,1,8192,128]{3,0,2,1:T(1,128)S(1)} %bitcast.242, f32[1,1,8192,128]{3,0,2,1:T(1,128)S(1)} %bitcast.241), kind=kLoop, calls=%fused_computation.23 | loop fusion | flops 6291456 | bytes 12582912
  146.4 9.1 %bitcast_dynamic-update-slice_fusion.2 = bf16[2,6,1,8192,128]{4,0,2,1,3:T(2,128)(2,1)} fusion(bf16[2,6,1,8192,128]{4,0,2,1,3:T(2,128)(2,1)} %bitcast_dynamic-update-slice_fusion.3, f32[1,1,8192,128]{3,0,2,1:T(1,128)S(1)} %bitcast.244, f32[1,1,8192,128]{3,0,2,1:T(1,128)S(1)} %bitcast.243), kind=kLoop, calls=%fused_computation.22 | loop fusion | flops 6291456 | bytes 12582912
  155.5 9.1 %bitcast_dynamic-update-slice_fusion.1 = bf16[2,6,1,8192,128]{4,0,2,1,3:T(2,128)(2,1)} fusion(bf16[2,6,1,8192,128]{4,0,2,1,3:T(2,128)(2,1)} %bitcast_dynamic-update-slice_fusion.2, f32[1,1,8192,128]{3,0,2,1:T(1,128)S(1)} %bitcast.246, f32[1,1,8192,128]{3,0,2,1:T(1,128)S(1)} %bitcast.245), kind=kLoop, calls=%fused_computation.21 | loop fusion | flops 6291456 | bytes 12582912
  164.6 9.2 %bitcast_dynamic-update-slice_fusion = bf16[2,6,1,8192,128]{4,0,2,1,3:T(2,128)(2,1)} fusion(bf16[2,6,1,8192,128]{4,0,2,1,3:T(2,128)(2,1)} %bitcast_dynamic-update-slice_fusion.1, f32[1,1,8192,128]{3,0,2,1:T(1,128)S(1)} %bitcast.248, f32[1,1,8192,128]{3,0,2,1:T(1,128)S(1)} %bitcast.247), kind=kLoop, calls=%fused_computation.20 | loop fusion | flops 6291456 | bytes 12582912
  173.7 9.1 %bitcast_dynamic-update-slice_fusion.5 = bf16[2,6,1,8192,128]{4,0,2,1,3:T(2,128)(2,1)} fusion(bf16[2,6,1,8192,128]{4,0,2,1,3:T(2,128)(2,1)} %bitcast_dynamic-update-slice_fusion, f32[1,1,8192,128]{3,0,2,1:T(1,128)S(1)} %bitcast.250, f32[1,1,8192,128]{3,0,2,1:T(1,128)S(1)} %bitcast.249), kind=kLoop, calls=%fused_computation.25 | loop fusion | flops 6291456 | bytes 12582912 | tf_op jit(solution)/shard_map/stack | solution.py:28
  182.9 282.7 %all_to_all.27 = bf16[2,6,1,8192,128]{4,0,2,1,3:T(2,128)(2,1)S(1)} all-to-all(bf16[2,6,1,8192,128]{4,0,2,1,3:T(2,128)(2,1)} %bitcast_dynamic-update-slice_fusion.5), channel_id=1, replica_groups=mesh['chan'=64,'win'=2] {'chan'}, dimensions={3} | all-to-all | bytes 50331648 | tf_op jit(solution)/shard_map/all_to_all | solution.py:32
  465.6 8.9 %copy.50 = bf16[2,6,64,128,128]{4,3,1,0,2:T(8,128)(2,1)} copy(bf16[2,6,64,128,128]{4,0,1,3,2:T(2,128)(2,1)S(1)} %bitcast.236) | data formatting | bytes 50331648
  474.4 26.9 %copy.59 = bf16[8,8,1536,128]{3,1,2,0:T(8,128)(2,1)} copy(bf16[8,8,1536,128]{3,2,1,0:T(8,128)(2,1)} %bitcast.237) | data formatting | bytes 50331648
  501.3 282.6 %reduce-scatter.5.cloned.1.call-done = bf16[32,196608]{1,0:T(8,128)(2,1)} async-done(((bf16[64,196608]{1,0:T(8,128)(2,1)}), bf16[32,196608]{1,0:T(8,128)(2,1)}) %reduce-scatter.5.cloned.1.call-update) | async-done | bytes 12582928
  783.9 7.4 copy.54
  791.2 5.1 copy.51
  (66 shorter events, 34.4 us)
Async XLA Ops:
  6.5 17.8 %copy-start.17 = (s32[6,64]{1,0:T(8,128)S(1)}, s32[6,64]{1,0:T(8,128)}, u32[]{:S(2)}) copy-start(s32[6,64]{1,0:T(8,128)} %param.7) | copy-start | bytes 4612
  12.0 31.8 %all-to-all-start = ((bf16[2,64,32,128]{3,2,0,1:T(8,128)(2,1)}), bf16[2,64,32,128]{3,2,0,1:T(8,128)(2,1)S(1)}, u32[]{:S(2)}, u32[]{:S(2)}) async-start(bf16[2,64,32,128]{3,2,0,1:T(8,128)(2,1)} %select_bitcast_fusion), calls=%async_computation | async-start | bytes 2097152 | tf_op jit(solution)/shard_map/all_to_all | solution.py:16
  24.3 759.6 %reduce-scatter.5.cloned.1.call-start = ((), (), s32[]{:S(2)}) async-start(), calls=%async_computation.3 | async-start | bytes 37748736
  61.9 5.4 copy-start.11
  70.4 5.5 copy-start.13
  79.1 5.6 copy-start.15
  87.7 5.5 copy-start.4
  93.2 2.2 copy-start.3
  95.4 2.2 copy-start.6
  97.6 2.2 copy-start.5
  99.8 2.2 copy-start.8
  99.8 2.5 copy-start.12
  102.3 2.2 copy-start.7
  104.5 2.2 copy-start.10
  104.5 2.5 copy-start.14
  106.9 2.2 copy-start.9
  109.1 1.2 copy-start.16
  155.5 9.1 %copy-start = (f32[64,128,128]{2,1,0:T(8,128)S(1)}, f32[64,128,128]{2,1,0:T(8,128)}, u32[]{:S(2)}) copy-start(f32[64,128,128]{2,1,0:T(8,128)} %convolution_subtract_fusion.1) | copy-start | bytes 12582916
  164.6 9.2 %copy-start.1 = (f32[64,128,128]{2,1,0:T(8,128)S(1)}, f32[64,128,128]{2,1,0:T(8,128)}, u32[]{:S(2)}) copy-start(f32[64,128,128]{2,1,0:T(8,128)} %convolution_add_fusion) | copy-start | bytes 12582916
  164.6 9.2 %copy-start.2 = (f32[64,128,128]{2,1,0:T(8,128)S(1)}, f32[64,128,128]{2,1,0:T(8,128)}, u32[]{:S(2)}) copy-start(f32[64,128,128]{2,1,0:T(8,128)} %convolution_subtract_fusion) | copy-start | bytes 12582916
Sparse Core Ops, SparseCore 0:
  501.4 282.3 reduce-scatter.4
where the time goes:
time: 805 us; the launch traced here: 803 us
  waiting for transfers between devices  302 us (38%)
  blocking collectives  283 us (35%)
  local copies, waits for them, and re-layouts  71.2 us (9%)
  other arithmetic  64.3 us (8%)
  matrix products  57.1 us (7%)
  between operations  13.7 us (2%)
  starting transfers between devices  12.3 us (2%)
    all_to_all x1, blocking collectives, body(): lax.all_to_all(partial_value, 'chan', split_axis=3, concat_axis=2, tiled=...  283 us
    unnamed x2, waiting for transfers between devices  283 us
    unnamed x40, local copies, waits for them, and re-layouts  58.9 us
    dot_general x24, matrix products, pair_products(): jnp.einsum('fwbi,fwbj->fbij', left, right, preferred_element_type=jnp.flo...  57.1 us
    unnamed x5, other arithmetic  45.6 us
    all_to_all x1, waiting for transfers between devices, body(): lax.all_to_all(selected, 'chan', split_axis=1, concat_axis=3, tiled=True)  19.3 us
  transfers between devices with their start and end apart: 2, of which 2 were waited for; matrix products, arithmetic and copies ran while one was open for 0% of the time, Pallas kernels for 0%

commit v1 on v0

v1 whole, which is shorter than its diff:
```python
import functools
import math

import jax
import jax.numpy as jnp
from jax import lax
from jax.experimental import pallas as pl
from jax.experimental.pallas import tpu as pltpu
from jax.sharding import PartitionSpec as P


def pair_kernel(scale, own_ref, part_ref, out_ref):
    rounds = part_ref.shape[2]
    channels = own_ref.shape[3]
    for b in range(own_ref.shape[1]):
        real, imag = own_ref[0, b], own_ref[1, b]
        left = jnp.concatenate(
            [jnp.concatenate([real, imag], 0).T, jnp.concatenate([imag, -real], 0).T], 0
        )
        for r in range(0, rounds, 2):
            right = jnp.concatenate(
                [
                    jnp.concatenate([part_ref[b, 0, q], part_ref[b, 1, q]], 0)
                    for q in (r, r + 1)
                ],
                1,
            )
            product = jnp.dot(left, right, preferred_element_type=jnp.float32) * scale
            product = product.astype(out_ref.dtype)
            for half in range(2):
                for q in range(2):
                    out_ref[half, r + q, b] = product[
                        half * channels : (half + 1) * channels,
                        q * channels : (q + 1) * channels,
                    ]


def pair_products(own, part, scale):
    bins, _, rounds, windows, channels = part.shape
    step = 2
    return pl.pallas_call(
        functools.partial(pair_kernel, scale),
        grid=(bins // step,),
        out_shape=jax.ShapeDtypeStruct((2, rounds, bins, channels, channels), own.dtype),
        in_specs=[
            pl.BlockSpec((2, step, windows, channels), lambda i: (0, i, 0, 0)),
            pl.BlockSpec((step, 2, rounds, windows, channels), lambda i: (i, 0, 0, 0, 0)),
        ],
        out_specs=pl.BlockSpec((2, rounds, step, channels, channels), lambda i: (0, 0, i, 0, 0)),
        compiler_params=pltpu.CompilerParams(vmem_limit_bytes=32 << 20),
        name="pair_products",
    )(own, part)


def body(spectra, freq_idx, pairing):
    nblocks = lax.axis_size("chan")
    nwin = lax.axis_size("win")
    rounds = pairing.shape[0]
    selected = jnp.take(spectra, freq_idx, axis=1)
    _, fbins, width, channels = selected.shape
    scale = 1.0 / math.sqrt(width * nwin)
    own = lax.all_to_all(selected, "win", split_axis=1, concat_axis=2, tiled=True)
    units = jnp.transpose(selected, (1, 0, 2, 3)).reshape(fbins * 2, width, channels)
    spread = lax.all_to_all(units, ("win", "chan"), split_axis=0, concat_axis=0, tiled=True)
    blocks = jnp.transpose(spread.reshape(nwin, nblocks, width, channels), (1, 0, 2, 3))
    wanted = jnp.take(blocks.reshape(nblocks, nwin * width, channels), pairing.T, axis=0)
    part = lax.all_to_all(wanted, "chan", split_axis=0, concat_axis=0, tiled=True)
    part = part.reshape(fbins // nwin, 2, rounds, nwin * width, channels)
    return pair_products(own, part, scale)


def solution(mesh):
    return jax.shard_map(
        body,
        mesh=mesh,
        in_specs=(P(None, None, "win", "chan"), P(), P()),
        out_specs=P(None, None, "win", "chan", None),
        check_vma=False,
    )
```

time: 805 us -> 160 us (0.20)
  blocking collectives: 283 us -> 0 us
  waiting for transfers between devices: 302 us -> 95.9 us
  matrix products: 57.1 us -> 0 us
  local copies, waits for them, and re-layouts: 71.2 us -> 16.9 us
  other arithmetic: 64.3 us -> 10.3 us
  Pallas kernels: 0 us -> 14.8 us
  between operations: 13.7 us -> 0.09 us
  starting transfers between devices: 12.3 us -> 21.2 us
    all_to_all x1 -> x0, blocking collectives: 283 us -> none  [body(): lax.all_to_all(partial_value, 'chan', split_axis=3, concat_axis=2, tiled=...]
    unnamed x2 -> x0, waiting for transfers between devices: 283 us -> none
    all_to_all x1 -> x3, waiting for transfers between devices: 19.3 us -> 95.9 us  [the longest x1 78.5 us: body(): lax.all_to_all(wanted, 'chan', split_axis=0, concat_axis=0, tiled=True)]
    unnamed x40 -> x2, local copies, waits for them, and re-layouts: 58.9 us -> 0.01 us
    dot_general x24 -> x0, matrix products: 57.1 us -> none  [pair_products(): jnp.einsum('fwbi,fwbj->fbij', left, right, preferred_element_type=jnp.flo...]
    unnamed x5 -> x0, other arithmetic: 45.6 us -> none
    pallas_call x0 -> x1, Pallas kernels: none -> 14.8 us  [pair_products(): pl.pallas_call(functools.partial(pair_kernel, scale), grid=(bins // step,...]
    another operation x1 -> x0, other arithmetic: 9.12 us -> none  [body(): jnp.stack(results, 1)]
  transfers between devices with their start and end apart: 2 -> 3, of which waited for: 2 -> 2; matrix products, arithmetic and copies ran while one was open for 0% -> 14% of each run, Pallas kernels for 0% -> 0%
where the time goes in v1:
time: 160 us; the launch traced here: 159 us
  waiting for transfers between devices  95.9 us (60%)
  starting transfers between devices  21.2 us (13%)
  local copies, waits for them, and re-layouts  16.9 us (11%)
  Pallas kernels  14.8 us (9%)
  other arithmetic  10.3 us (6%)
    all_to_all x1, waiting for transfers between devices, body(): lax.all_to_all(wanted, 'chan', split_axis=0, concat_axis=0, tiled=True)  78.5 us
    all_to_all x1, waiting for transfers between devices, body(): lax.all_to_all(units, ('win', 'chan'), split_axis=0, concat_axis=0, tiled...  17.4 us
    pallas_call x1, Pallas kernels, pair_products(): pl.pallas_call(functools.partial(pair_kernel, scale), grid=(bins // step,...  14.8 us
    gather x1, local copies, waits for them, and re-layouts, body(): jnp.take(blocks.reshape(nblocks, nwin * width, channels), pairing.T, axis=0)  13.3 us
    all_to_all x1, starting transfers between devices, body(): lax.all_to_all(units, ('win', 'chan'), split_axis=0, concat_axis=0, tiled...  11.5 us
    select_n x2, other arithmetic, body(): jnp.take(blocks.reshape(nblocks, nwin * width, channels), pairing.T, axis=0)  6.69 us
    all_to_all x1, starting transfers between devices, body(): lax.all_to_all(wanted, 'chan', split_axis=0, concat_axis=0, tiled=True)  6.14 us
    all_to_all x1, starting transfers between devices, body(): lax.all_to_all(selected, 'win', split_axis=1, concat_axis=2, tiled=True)  3.58 us
  transfers between devices with their start and end apart: 3, of which 2 were waited for; matrix products, arithmetic and copies ran while one was open for 14% of the time, Pallas kernels for 0%

profile of v1, /device:TPU:1, one launch (start us, length us, event | category | flops | bytes accessed | tf_op | source)
XLA Modules:
  0.0 159.3 jit_solution(6886617290516912314)
XLA Ops:
  0.0 0.0 copy-start
  0.0 0.7 compare_and_fusion.1
  0.7 0.7 compare_select_fusion.1
  1.3 2.9 %gather_fusion = bf16[64,2,32,128]{3,2,1,0:T(8,128)(2,1)S(1)} fusion(bf16[2,256,32,128]{3,2,1,0:T(8,128)(2,1)} %param.3, s32[1024]{0:T(1024)S(1)} %pad_clamp_fusion.1), kind=kCustom, calls=%fused_computation | custom fusion | bytes 2097408 | tf_op jit(solution)/shard_map/jit(_take)/gather | solution.py:59
  4.3 1.1 broadcast_select_fusion.1
  5.4 11.5 %all-to-all-start.1 = ((bf16[128,32,128]{2,1,0:T(8,128)(2,1)}), bf16[128,32,128]{2,1,0:T(8,128)(2,1)S(1)}, u32[]{:S(2)}, u32[]{:S(2)}) async-start(bf16[128,32,128]{2,1,0:T(8,128)(2,1)} %bitcast.5), calls=%async_computation.1 | async-start | bytes 2097152 | tf_op jit(solution)/shard_map/all_to_all | solution.py:64
  16.9 0.0 copy-done
  17.0 0.1 copy.10
  17.1 0.1 copy.12
  17.2 0.1 reshape.36
  17.3 1.1 fusion
  18.5 17.4 %all-to-all-done.1 = bf16[128,32,128]{2,1,0:T(8,128)(2,1)S(1)} async-done(((bf16[128,32,128]{2,1,0:T(8,128)(2,1)}), bf16[128,32,128]{2,1,0:T(8,128)(2,1)S(1)}, u32[]{:S(2)}, u32[]{:S(2)}) %all-to-all-start.1) | async-done | bytes 1048608 | tf_op jit(solution)/shard_map/all_to_all | solution.py:64
  35.9 3.6 %all-to-all-start = ((bf16[2,64,32,128]{3,2,0,1:T(8,128)(2,1)}), bf16[2,64,32,128]{3,2,0,1:T(8,128)(2,1)S(1)}, u32[]{:S(2)}, u32[]{:S(2)}) async-start(bf16[2,64,32,128]{3,2,0,1:T(8,128)(2,1)} %fusion), calls=%async_computation | async-start | bytes 2097152 | tf_op jit(solution)/shard_map/all_to_all | solution.py:62
  39.4 0.1 copy.11
  39.6 13.3 %gather_fusion.1 = bf16[384,64,128]{2,1,0:T(8,128)(2,1)} fusion(bf16[64,64,128]{2,1,0:T(8,128)(2,1)S(1)} %bitcast.18, s32[1024]{0:T(1024)S(1)} %pad_clamp_fusion), kind=kCustom, calls=%fused_computation.1 | custom fusion | bytes 12584448 | tf_op jit(solution)/shard_map/jit(_take)/gather | solution.py:66
  52.9 6.7 %broadcast_select_fusion = bf16[64,6,64,128]{3,2,1,0:T(8,128)(2,1)} fusion(bf16[64,6,64,128]{3,2,1,0:T(8,128)(2,1)} %bitcast.19, pred[64,6]{1,0:T(8,128)(4,1)S(1)} %copy.10), kind=kLoop, calls=%fused_computation.2 | loop fusion | flops 3145728 | bytes 12583296 | tf_op jit(solution)/shard_map/jit(_take)/select_n | solution.py:66
  59.6 0.0 all-to-all-done
  59.6 6.1 %all-to-all-start.2 = ((bf16[64,6,64,128]{3,2,1,0:T(8,128)(2,1)}), bf16[64,6,64,128]{3,2,1,0:T(8,128)(2,1)}, u32[]{:S(2)}, u32[]{:S(2)}) async-start(bf16[64,6,64,128]{3,2,1,0:T(8,128)(2,1)} %broadcast_select_fusion), calls=%async_computation.2 | async-start | bytes 12582912 | tf_op jit(solution)/shard_map/all_to_all | solution.py:67
  65.8 0.2 copy.9
  65.9 78.5 %all-to-all-done.2 = bf16[64,6,64,128]{3,2,1,0:T(8,128)(2,1)} async-done(((bf16[64,6,64,128]{3,2,1,0:T(8,128)(2,1)}), bf16[64,6,64,128]{3,2,1,0:T(8,128)(2,1)}, u32[]{:S(2)}, u32[]{:S(2)}) %all-to-all-start.2) | async-done | bytes 6291488 | tf_op jit(solution)/shard_map/all_to_all | solution.py:67
  144.4 14.8 %pair_products.1 = bf16[2,6,32,128,128]{4,3,2,1,0:T(8,128)(2,1)} custom-call(bf16[2,32,64,128]{3,2,1,0:T(8,128)(2,1)S(1)} %bitcast.17, bf16[32,2,6,64,128]{4,3,2,1,0:T(8,128)(2,1)} %bitcast.10.part_ref), custom_call_target="tpu_custom_call" | custom-call | tf_op jit(solution)/shard_map/pair_products/pallas_call | solution.py:41
  (4 shorter events, 0.0 us)
Async XLA Ops:
  0.0 16.9 %copy-start = (s32[6,64]{1,0:T(8,128)S(1)}, s32[6,64]{1,0:T(8,128)}, u32[]{:S(2)}) copy-start(s32[6,64]{1,0:T(8,128)} %param.5) | copy-start | bytes 4612
  5.4 30.4 %all-to-all-start.1 = ((bf16[128,32,128]{2,1,0:T(8,128)(2,1)}), bf16[128,32,128]{2,1,0:T(8,128)(2,1)S(1)}, u32[]{:S(2)}, u32[]{:S(2)}) async-start(bf16[128,32,128]{2,1,0:T(8,128)(2,1)} %bitcast.5), calls=%async_computation.1 | async-start | bytes 2097152 | tf_op jit(solution)/shard_map/all_to_all | solution.py:64
  35.9 23.7 %all-to-all-start = ((bf16[2,64,32,128]{3,2,0,1:T(8,128)(2,1)}), bf16[2,64,32,128]{3,2,0,1:T(8,128)(2,1)S(1)}, u32[]{:S(2)}, u32[]{:S(2)}) async-start(bf16[2,64,32,128]{3,2,0,1:T(8,128)(2,1)} %fusion), calls=%async_computation | async-start | bytes 2097152 | tf_op jit(solution)/shard_map/all_to_all | solution.py:62
  59.6 84.8 %all-to-all-start.2 = ((bf16[64,6,64,128]{3,2,1,0:T(8,128)(2,1)}), bf16[64,6,64,128]{3,2,1,0:T(8,128)(2,1)}, u32[]{:S(2)}, u32[]{:S(2)}) async-start(bf16[64,6,64,128]{3,2,1,0:T(8,128)(2,1)} %broadcast_select_fusion), calls=%async_computation.2 | async-start | bytes 12582912 | tf_op jit(solution)/shard_map/all_to_all | solution.py:67

commit v2 on v1

v2 whole, which is shorter than its diff:
```python
import functools
import math

import jax
import jax.numpy as jnp
from jax import lax
from jax.experimental import pallas as pl
from jax.experimental.pallas import tpu as pltpu
from jax.sharding import PartitionSpec as P

MESH = pl.DeviceIdType.MESH


def block_of(x, zh, y, c):
    return ((x * 2 + zh) * 4 + y) * 2 + c


def place(x, zh, w, y, c):
    return {"chan": block_of(x, zh, y, c), "win": w}


def move_kernel(
    spectra, freq, pairing, part, own,
    whole, sel, held_a, held_b, half_c, held_c, stage,
    load_sem, spread_send, spread_recv, ring_send, ring_recv,
    own_send, own_recv, part_send, part_recv,
):
    chan = lax.axis_index("chan")
    w = lax.axis_index("win")
    c = chan % 2
    y = (chan // 2) % 4
    zh = (chan // 8) % 2
    x = chan // 16
    rounds = pairing.shape[0]

    load = pltpu.make_async_copy(spectra, whole, load_sem)
    load.start()

    barrier = pltpu.get_barrier_semaphore()

    def greet(dx, dz, dy, dc):
        z = (zh * 2 + w + dz) % 4
        pl.semaphore_signal(
            barrier, inc=1, device_id=place((x + dx) % 4, z // 2, z % 2, (y + dy) % 4, (c + dc) % 2),
            device_id_type=MESH,
        )

    def greet_plane(o, carry):
        dc, one, two = o % 2, (o // 2) % 4, o // 8
        greet(0, one, two, dc)

        @pl.when(two > 0)
        def _():
            greet(two, one, 0, dc)

        @pl.when((one > 0) & (two > 0))
        def _():
            greet(one, 0, two, dc)

        return carry

    lax.fori_loop(1, 32, greet_plane, 0)
    load.wait()

    def pick(k, carry):
        f = freq[k]
        for part_index in range(2):
            sel[part_index, k // 32, k % 32] = whole[part_index, f]
        return carry

    lax.fori_loop(0, 64, pick, 0)
    pl.semaphore_wait(barrier, 31 + 24 + 18)

    def send(src, dst, ssem, rsem, target):
        pltpu.make_async_remote_copy(
            src_ref=src, dst_ref=dst, send_sem=ssem, recv_sem=rsem, device_id=target, device_id_type=MESH
        ).start()

    mine_a = block_of(x, zh, y, c)
    mine_b = y * 16 + (x * 2 + zh) * 2 + c
    mine_c = (x * 4 + y) * 2 + c

    def src_a(zh2, w2, y2):
        return sel.at[zh2, w2, pl.ds(2 * y2, 2)]

    def src_b(zh2, w2, x2):
        return sel.at[zh2, w2, pl.ds(8 + 2 * x2, 2)]

    def spread_a(o):
        zh2, w2, y2 = (zh + o) % 2, (w + o // 2) % 2, (y + o // 4) % 4
        send(src_a(zh2, w2, y2), held_a.at[mine_a], spread_send.at[0], spread_recv.at[0], place(x, zh2, w2, y2, w))

    def spread_b(o):
        zh2, w2, x2 = (zh + o) % 2, (w + o // 2) % 2, (x + o // 4) % 4
        send(src_b(zh2, w2, x2), held_b.at[mine_b], spread_send.at[1], spread_recv.at[1], place(x2, zh2, w2, y, w))

    def spread_c(o):
        x2, y2, c2 = (x + o // 8) % 4, (y + o // 2) % 4, (c + o) % 2
        send(
            sel.at[c2, :, 16 + x2 * 4 + y2], half_c.at[:, mine_c],
            spread_send.at[2], spread_recv.at[2], place(x2, zh, w, y2, c2),
        )

    def spread(i, carry):
        spread_a((i * 5) % 16)
        spread_b((i * 7) % 16)
        spread_c((i * 2 * 5 + 1) % 32)
        spread_c((i * 2 * 7) % 32)
        return carry

    lax.fori_loop(1, 16, spread, 0)
    spread_c(1)
    pltpu.make_async_copy(sel.at[c, :, 16 + x * 4 + y], half_c.at[:, mine_c], spread_recv.at[2]).start()

    @pl.when(c == w)
    def _():
        pltpu.make_async_copy(src_a(zh, w, y), held_a.at[mine_a], spread_recv.at[0]).start()
        pltpu.make_async_copy(src_b(zh, w, x), held_b.at[mine_b], spread_recv.at[1]).start()

    @pl.when(c != w)
    def _():
        spread_a(0)
        spread_b(0)

    def arrived(ref, sem):
        pltpu.make_async_copy(ref, ref, sem).wait()

    block_a = held_a.at[pl.ds(x * 16, 16)]
    arrived(block_a, spread_recv.at[0])
    for d in (1, 3, 2):
        send(block_a, block_a, ring_send.at[0], ring_recv.at[0], place((x + d) % 4, zh, w, y, c))
    block_b = held_b.at[pl.ds(y * 16, 16)]
    arrived(block_b, spread_recv.at[1])
    for d in (1, 3, 2):
        send(block_b, block_b, ring_send.at[1], ring_recv.at[1], place(x, zh, w, (y + d) % 4, c))
    arrived(half_c, spread_recv.at[2])
    block_c = held_c.at[w, pl.ds(zh * 32, 32)]
    for dzh, dw in ((0, 1), (1, 1), (1, 0)):
        zh2, w2 = (zh + dzh) % 2, (w + dw) % 2
        send(half_c.at[w2], block_c, ring_send.at[2], ring_recv.at[2], place(x, zh2, w2, y, c))
    pltpu.make_async_copy(half_c.at[w], block_c, ring_recv.at[2]).start()

    send(sel.at[:, 1 - w], own.at[:, :, w], own_send, own_recv, place(x, zh, 1 - w, y, c))
    pltpu.make_async_copy(sel.at[:, w], own.at[:, :, w], own_recv).start()

    arrived(held_a.at[pl.ds(0, 48)], ring_recv.at[0])
    arrived(held_b.at[pl.ds(0, 48)], ring_recv.at[1])
    arrived(held_c, ring_recv.at[2])

    bin_c = x * 4 + y

    def fill_a(slot, r, b):
        stage[slot] = held_a[pairing[r, b]]
        return part.at[y, zh, r, :, c]

    def fill_b(slot, r, b):
        p = pairing[r, b]
        stage[slot] = held_b[((p // 2) % 4) * 16 + (p // 8) * 2 + p % 2]
        return part.at[4 + x, zh, r, :, c]

    def fill_c(slot, r, b):
        p = pairing[r, b]
        at = ((p // 8) % 2) * 32 + (p // 16) * 8 + p % 8
        stage[slot, 0] = held_c[0, at]
        stage[slot, 1] = held_c[1, at]
        return part.at[8 + bin_c // 2, c, r, bin_c % 2]

    def give(slot, dst, target):
        send(stage.at[slot], dst, part_send, part_recv, target)

    def give_a(slot, r, o):
        zh2, y2, c2 = (zh + o) % 2, (y + o // 2) % 4, (c + o // 8) % 2
        give(slot, fill_a(slot, r, block_of(x, zh2, y2, c2)), place(x, zh2, w, y2, c2))

    def give_b(slot, r, o):
        zh2, x2, c2 = (zh + o) % 2, (x + o // 2) % 4, (c + o // 8) % 2
        give(slot, fill_b(slot, r, block_of(x2, zh2, y, c2)), place(x2, zh2, w, y, c2))

    def give_c(slot, r, o):
        x2, y2, c2 = (x + o // 8) % 4, (y + o // 2) % 4, (c + o) % 2
        give(slot, fill_c(slot, r, block_of(x2, zh, y2, c2)), place(x2, zh, w, y2, c2))

    def give_round(r, carry):
        def step(i, carry):
            slot = (r * 15 + i - 1) * 4
            give_a(slot, r, (i * 5) % 16)
            give_c(slot + 1, r, (i * 2 * 5 + 1) % 32)
            give_b(slot + 2, r, (i * 7) % 16)
            give_c(slot + 3, r, (i * 2 * 7) % 32)
            return carry

        lax.fori_loop(1, 16, step, 0)
        give_c(rounds * 60 + r, r, 1)
        slot = rounds * 61 + r * 3
        for n, fill in enumerate((fill_a, fill_b, fill_c)):
            pltpu.make_async_copy(stage.at[slot + n], fill(slot + n, r, chan), part_recv).start()
        return carry

    lax.fori_loop(0, rounds, give_round, 0)

    arrived(half_c.at[:, pl.ds(0, 31)], spread_send.at[2])
    for n in range(2):
        @pl.when(c == w)
        def _():
            arrived(held_a.at[pl.ds(0, 15)], spread_send.at[n])

        @pl.when(c != w)
        def _():
            arrived(held_a.at[pl.ds(0, 16)], spread_send.at[n])

        arrived(held_a.at[pl.ds(0, 48)], ring_send.at[n])
    arrived(held_a.at[pl.ds(0, 48)], ring_send.at[2])
    arrived(sel.at[:, 0], own_send)
    arrived(sel, own_recv)
    arrived(stage.at[pl.ds(0, rounds * 61)], part_send)
    arrived(stage, part_recv)


def move(spectra, freq_idx, pairing):
    _, _, width, channels = spectra.shape
    rounds = pairing.shape[0]
    kind = spectra.dtype
    unit = (width, channels)
    return pl.pallas_call(
        move_kernel,
        out_shape=(
            jax.ShapeDtypeStruct((16, 2, rounds, 2, 2) + unit, kind),
            jax.ShapeDtypeStruct((2, 32, 2) + unit, kind),
        ),
        in_specs=[
            pl.BlockSpec(memory_space=pl.ANY),
            pl.BlockSpec(memory_space=pltpu.SMEM),
            pl.BlockSpec(memory_space=pltpu.SMEM),
        ],
        out_specs=(pl.BlockSpec(memory_space=pl.ANY), pl.BlockSpec(memory_space=pl.ANY)),
        scratch_shapes=[
            pltpu.VMEM(spectra.shape, kind),
            pltpu.VMEM((2, 2, 32) + unit, kind),
            pltpu.VMEM((64, 2) + unit, kind),
            pltpu.VMEM((64, 2) + unit, kind),
            pltpu.VMEM((2, 32) + unit, kind),
            pltpu.VMEM((2, 64) + unit, kind),
            pltpu.VMEM((rounds * 64, 2) + unit, kind),
            pltpu.SemaphoreType.DMA,
            pltpu.SemaphoreType.DMA((3,)),
            pltpu.SemaphoreType.DMA((3,)),
            pltpu.SemaphoreType.DMA((3,)),
            pltpu.SemaphoreType.DMA((3,)),
            pltpu.SemaphoreType.DMA,
            pltpu.SemaphoreType.DMA,
            pltpu.SemaphoreType.DMA,
            pltpu.SemaphoreType.DMA,
        ],
        compiler_params=pltpu.CompilerParams(
            collective_id=0, has_side_effects=True, vmem_limit_bytes=32 << 20
        ),
        name="move",
    )(spectra, freq_idx, pairing)


def pair_kernel(scale, own_ref, part_ref, out_ref):
    rounds = part_ref.shape[2]
    channels = own_ref.shape[3]
    for b in range(own_ref.shape[1]):
        real, imag = own_ref[0, b], own_ref[1, b]
        left = jnp.concatenate(
            [jnp.concatenate([real, imag], 0).T, jnp.concatenate([imag, -real], 0).T], 0
        )
        for r in range(0, rounds, 2):
            right = jnp.concatenate(
                [
                    jnp.concatenate([part_ref[0, 0, q, b], part_ref[0, 1, q, b]], 0)
                    for q in (r, r + 1)
                ],
                1,
            )
            product = jnp.dot(left, right, preferred_element_type=jnp.float32) * scale
            product = product.astype(out_ref.dtype)
            for half in range(2):
                for q in range(2):
                    out_ref[half, r + q, b] = product[
                        half * channels : (half + 1) * channels,
                        q * channels : (q + 1) * channels,
                    ]


def pair_products(own, part, scale):
    groups, _, rounds, step, windows, channels = part.shape
    return pl.pallas_call(
        functools.partial(pair_kernel, scale),
        grid=(groups,),
        out_shape=jax.ShapeDtypeStruct((2, rounds, groups * step, channels, channels), own.dtype),
        in_specs=[
            pl.BlockSpec((2, step, windows, channels), lambda i: (0, i, 0, 0)),
            pl.BlockSpec((1, 2, rounds, step, windows, channels), lambda i: (i, 0, 0, 0, 0, 0)),
        ],
        out_specs=pl.BlockSpec((2, rounds, step, channels, channels), lambda i: (0, 0, i, 0, 0)),
        compiler_params=pltpu.CompilerParams(vmem_limit_bytes=32 << 20),
        name="pair_products",
    )(own, part)


def body(spectra, freq_idx, pairing):
    _, _, width, channels = spectra.shape
    rounds = pairing.shape[0]
    scale = 1.0 / math.sqrt(width * lax.axis_size("win"))
    part, own = move(spectra, freq_idx, pairing)
    own = own.reshape(2, 32, 2 * width, channels)
    part = part.reshape(16, 2, rounds, 2, 2 * width, channels)
    return pair_products(own, part, scale)


def solution(mesh):
    return jax.shard_map(
        body,
        mesh=mesh,
        in_specs=(P(None, None, "win", "chan"), P(), P()),
        out_specs=P(None, None, "win", "chan", None),
        check_vma=False,
    )
```

time: 160 us -> 105 us (0.66)
  waiting for transfers between devices: 95.9 us -> 0 us
  Pallas kernels: 14.8 us -> 102 us
  starting transfers between devices: 21.2 us -> 0 us
  local copies, waits for them, and re-layouts: 16.9 us -> 3.53 us
  other arithmetic: 10.3 us -> 0 us
    all_to_all x3 -> x0, waiting for transfers between devices: 95.9 us -> none  [the longest x1 78.5 us: body(): lax.all_to_all(wanted, 'chan', split_axis=0, concat_axis=0, tiled=True)]
    pallas_call x1 -> x2, Pallas kernels: 14.8 us -> 102 us  [the longest x1 91 us: move(): pl.pallas_call(move_kernel, out_shape=(jax.ShapeDtypeStruct((16, 2, round...]
    all_to_all x3 -> x0, starting transfers between devices: 21.2 us -> none  [the longest x1 11.5 us: body(): lax.all_to_all(units, ('win', 'chan'), split_axis=0, concat_axis=0, tiled...]
    gather x2 -> x0, local copies, waits for them, and re-layouts: 16.3 us -> none  [the longest x1 13.3 us: body(): jnp.take(blocks.reshape(nblocks, nwin * width, channels), pairing.T, axis=0)]
    select_n x5 -> x0, other arithmetic: 9.62 us -> none  [the longest x2 6.69 us: body(): jnp.take(blocks.reshape(nblocks, nwin * width, channels), pairing.T, axis=0)]
    unnamed x2 -> x6, local copies, waits for them, and re-layouts: 0.01 us -> 3.53 us
  transfers between devices with their start and end apart: 3 -> 0, of which waited for: 2 -> 0; matrix products, arithmetic and copies ran while one was open for 14% -> 0% of each run, Pallas kernels for 0% -> 0%
where the time goes in v2:
time: 105 us
  Pallas kernels  102 us (97%)
  local copies, waits for them, and re-layouts  3.53 us (3%)
    pallas_call x1, Pallas kernels, move(): pl.pallas_call(move_kernel, out_shape=(jax.ShapeDtypeStruct((16, 2, round...  91 us
    pallas_call x1, Pallas kernels, pair_products(): pl.pallas_call(functools.partial(pair_kernel, scale), grid=(groups,), out...  10.6 us
    unnamed x6, local copies, waits for them, and re-layouts  3.53 us

profile of v2, /device:TPU:1, one launch (start us, length us, event | category | flops | bytes accessed | tf_op | source)
XLA Modules:
  0.0 105.1 jit_solution(10625434929785570353)
XLA Ops:
  0.0 0.0 copy-start
  0.0 2.2 %copy-done = bf16[2,256,32,128]{3,2,1,0:T(8,128)(2,1)S(1)} copy-done((bf16[2,256,32,128]{3,2,1,0:T(8,128)(2,1)S(1)}, bf16[2,256,32,128]{3,2,1,0:T(8,128)(2,1)}, u32[]{:S(2)}) %copy-start) | copy-done | bytes 4194328
  2.2 0.0 copy-start.1
  2.2 0.7 copy-done.1
  2.9 0.0 copy-start.2
  2.9 0.7 copy-done.2
  3.5 91.0 %move.1 = (bf16[16,2,6,2,2,32,128]{6,5,4,3,2,1,0:T(8,128)(2,1)S(1)}, bf16[2,32,2,32,128]{4,3,2,1,0:T(8,128)(2,1)S(1)}) custom-call(bf16[2,256,32,128]{3,2,1,0:T(8,128)(2,1)S(1)} %copy-done, s32[64]{0:T(128)S(1)} %copy-done.2, s32[6,64]{1,0:T(8,128)S(1)} %copy-done.1), custom_call_target="tpu_custom_call" | custom-call | tf_op jit(solution)/shard_map/move/pallas_call | solution.py:224
  94.5 10.6 %pair_products.1 = bf16[2,6,32,128,128]{4,3,2,1,0:T(8,128)(2,1)} custom-call(bf16[2,32,64,128]{3,2,1,0:T(8,128)(2,1)S(1)} %bitcast.3, bf16[16,2,6,2,64,128]{5,4,3,2,1,0:T(8,128)(2,1)S(1)} %bitcast.2), custom_call_target="tpu_custom_call" | custom-call | tf_op jit(solution)/shard_map/pair_products/pallas_call | solution.py:289
Async XLA Ops:
  0.0 2.2 %copy-start = (bf16[2,256,32,128]{3,2,1,0:T(8,128)(2,1)S(1)}, bf16[2,256,32,128]{3,2,1,0:T(8,128)(2,1)}, u32[]{:S(2)}) copy-start(bf16[2,256,32,128]{3,2,1,0:T(8,128)(2,1)} %spectra.1) | copy-start | bytes 12582916
  2.2 0.7 copy-start.1
  2.9 0.7 copy-start.2

commit v3 on v2

v3 whole, which is shorter than its diff:
```python
import functools
import math

import jax
import jax.numpy as jnp
from jax import lax
from jax.experimental import pallas as pl
from jax.experimental.pallas import tpu as pltpu
from jax.sharding import PartitionSpec as P

MESH = pl.DeviceIdType.MESH


def block_of(x, zh, y, c):
    return ((x * 2 + zh) * 4 + y) * 2 + c


def place(x, zh, w, y, c):
    return {"chan": block_of(x, zh, y, c), "win": w}


AHEAD = 4
C_STEP = 4


def move_kernel(
    spectra, freq_in, pairing_in, part, left, done,
    whole, freq, pairing, sel, own, held_a, held_b, half_c, held_c, stage,
    load_sem, spread_send, spread_recv, ring_send, ring_recv, far_send, far_recv,
    own_send, own_recv, part_send, part_recv,
):
    chan = lax.axis_index("chan")
    w = lax.axis_index("win")
    c = chan % 2
    y = (chan // 2) % 4
    zh = (chan // 8) % 2
    x = chan // 16
    rounds = pairing.shape[0]

    loads = [
        pltpu.make_async_copy(src, dst, load_sem.at[n])
        for n, (src, dst) in enumerate(((spectra, whole), (freq_in, freq), (pairing_in, pairing)))
    ]
    for load in loads:
        load.start()

    barrier = pltpu.get_barrier_semaphore()

    def greet(dx, dz, dy, dc):
        z = (zh * 2 + w + dz) % 4
        pl.semaphore_signal(
            barrier, inc=1, device_id=place((x + dx) % 4, z // 2, z % 2, (y + dy) % 4, (c + dc) % 2),
            device_id_type=MESH,
        )

    def greet_plane(o, carry):
        dc, one, two = o % 2, (o // 2) % 4, o // 8
        greet(0, one, two, dc)

        @pl.when(two > 0)
        def _():
            greet(two, one, 0, dc)

        @pl.when((one > 0) & (two > 0))
        def _():
            greet(one, 0, two, dc)

        return carry

    lax.fori_loop(1, 32, greet_plane, 0)
    for load in loads:
        load.wait()

    def pick(k, carry):
        f = freq[k]
        for half in range(2):
            sel[half, k // 32, k % 32] = whole[half, f]
        return carry

    lax.fori_loop(0, 64, pick, 0)
    pl.semaphore_wait(barrier, 31 + 24 + 18)

    def send(src, dst, ssem, rsem, target):
        pltpu.make_async_remote_copy(
            src_ref=src, dst_ref=dst, send_sem=ssem, recv_sem=rsem, device_id=target, device_id_type=MESH
        ).start()

    def arrived(ref, sem):
        pltpu.make_async_copy(ref, ref, sem).wait()

    mine_a = block_of(x, zh, y, c)
    mine_b = y * 16 + (x * 2 + zh) * 2 + c
    mine_c = (x * 4 + y) * 2 + c

    def src_a(zh2, w2, y2):
        return sel.at[zh2, w2, pl.ds(2 * y2, 2)]

    def src_b(zh2, w2, x2):
        return sel.at[zh2, w2, pl.ds(8 + 2 * x2, 2)]

    def spread_a(o):
        zh2, w2, y2 = (zh + o) % 2, (w + o // 2) % 2, (y + o // 4) % 4
        send(src_a(zh2, w2, y2), held_a.at[mine_a], spread_send.at[0], spread_recv.at[0], place(x, zh2, w2, y2, w))

    def spread_b(o):
        zh2, w2, x2 = (zh + o) % 2, (w + o // 2) % 2, (x + o // 4) % 4
        send(src_b(zh2, w2, x2), held_b.at[mine_b], spread_send.at[1], spread_recv.at[1], place(x2, zh2, w2, y, w))

    def spread_c(o):
        x2, y2, c2 = (x + o // 8) % 4, (y + o // 2) % 4, (c + o) % 2
        send(
            sel.at[c2, :, 16 + x2 * 4 + y2], half_c.at[:, mine_c],
            spread_send.at[2], spread_recv.at[2], place(x2, zh, w, y2, c2),
        )

    def spread_first(i, carry):
        spread_c((i * 5) % 32)
        return carry

    def spread_rest(i, carry):
        spread_a((i * 5) % 16)
        spread_b((i * 7) % 16)
        return carry

    lax.fori_loop(1, 32, spread_first, 0)
    pltpu.make_async_copy(sel.at[c, :, 16 + x * 4 + y], half_c.at[:, mine_c], spread_recv.at[2]).start()
    lax.fori_loop(1, 16, spread_rest, 0)

    @pl.when(c == w)
    def _():
        pltpu.make_async_copy(src_a(zh, w, y), held_a.at[mine_a], spread_recv.at[0]).start()
        pltpu.make_async_copy(src_b(zh, w, x), held_b.at[mine_b], spread_recv.at[1]).start()

    @pl.when(c != w)
    def _():
        spread_a(0)
        spread_b(0)

    arrived(half_c, spread_recv.at[2])
    block_c = held_c.at[w, pl.ds(zh * 32, 32)]
    for dzh, dw in ((1, 0), (0, 1), (1, 1)):
        zh2, w2 = (zh + dzh) % 2, (w + dw) % 2
        send(half_c.at[w2], block_c, ring_send.at[2], ring_recv.at[4], place(x, zh2, w2, y, c))
    pltpu.make_async_copy(half_c.at[w], block_c, ring_recv.at[4]).start()

    def at_a(d):
        return place((x + d) % 4, zh, w, y, c)

    def at_b(d):
        return place(x, zh, w, (y + d) % 4, c)

    groups = ((held_a, x, at_a), (held_b, y, at_b))
    for n, (held, at, target) in enumerate(groups):
        block = held.at[pl.ds(at * 16, 16)]
        arrived(block, spread_recv.at[n])
        for k, d in enumerate((1, 3)):
            send(block, block, ring_send.at[n], ring_recv.at[2 * n + k], target(d))

    send(sel.at[:, 1 - w], own.at[:, :, w], own_send, own_recv, place(x, zh, 1 - w, y, c))
    pltpu.make_async_copy(sel.at[:, w], own.at[:, :, w], own_recv).start()

    bin_c = x * 4 + y

    def fill_a(slot, r, b):
        stage[slot] = held_a[pairing[r, b]]
        return part.at[r // 2, y, zh, r % 2, :, c]

    def fill_b(slot, r, b):
        p = pairing[r, b]
        stage[slot] = held_b[((p // 2) % 4) * 16 + (p // 8) * 2 + p % 2]
        return part.at[r // 2, 4 + x, zh, r % 2, :, c]

    def fill_c(slot, r, b):
        p = pairing[r, b]
        at = ((p // 8) % 2) * 32 + (p // 16) * 8 + p % 8
        stage[slot, 0] = held_c[0, at]
        stage[slot, 1] = held_c[1, at]
        return part.at[r // 2, 8 + bin_c // 2, c, r % 2, bin_c % 2]

    def give(slot, r, dst, target):
        send(stage.at[slot], dst, part_send, part_recv.at[r // 2], target)

    def give_a(j):
        r, o = j // 15, ((j % 15 + 1) * 5) % 16
        slot = rounds * 31 + j
        zh2, y2, c2 = (zh + o) % 2, (y + o // 2) % 4, (c + o // 8) % 2
        give(slot, r, fill_a(slot, r, block_of(x, zh2, y2, c2)), place(x, zh2, w, y2, c2))

    def give_b(j):
        r, o = j // 15, ((j % 15 + 1) * 7) % 16
        slot = rounds * 46 + j
        zh2, x2, c2 = (zh + o) % 2, (x + o // 2) % 4, (c + o // 8) % 2
        give(slot, r, fill_b(slot, r, block_of(x2, zh2, y, c2)), place(x2, zh2, w, y, c2))

    def give_c(j):
        r, o = j // 31, ((j % 31 + 1) * 5) % 32
        x2, y2, c2 = (x + o // 8) % 4, (y + o // 2) % 4, (c + o) % 2
        give(j, r, fill_c(j, r, block_of(x2, zh, y2, c2)), place(x2, zh, w, y2, c2))

    def keep(r, carry):
        slot = rounds * 61 + r * 3
        for n, fill in enumerate((fill_a, fill_b, fill_c)):
            pltpu.make_async_copy(stage.at[slot + n], fill(slot + n, r, chan), part_recv.at[r // 2]).start()
        return carry

    def give_first(j, carry):
        give_c(j)
        return carry

    first = rounds * 31 - rounds * 5 * C_STEP

    def give_rest(i, carry):
        for n in range(max(3, C_STEP)):
            if n < 3:
                give_a(3 * i + n)
            if n < C_STEP:
                give_c(first + C_STEP * i + n)
            if n < 3:
                give_b(3 * i + n)
        return carry

    for n, (held, at, target) in enumerate(groups):
        for k, d in enumerate((3, 1)):
            arrived(held.at[pl.ds(((at + d) % 4) * 16, 16)], ring_recv.at[2 * n + k])
            half = held.at[pl.ds(((at + d) % 4) * 16 + 8 * k, 8)]
            send(half, half, far_send.at[n], far_recv.at[n], target(4 - d))

    arrived(held_c, ring_recv.at[4])
    lax.fori_loop(0, first, give_first, 0)
    arrived(held_a.at[pl.ds(0, 16)], far_recv.at[0])
    arrived(held_b.at[pl.ds(0, 16)], far_recv.at[1])
    lax.fori_loop(0, rounds * 5, give_rest, 0)
    lax.fori_loop(0, rounds, keep, 0)

    arrived(sel, own_recv)

    def turn(k, carry):
        real = own[0, k].reshape(-1, own.shape[-1])
        imag = own[1, k].reshape(-1, own.shape[-1])
        channels = real.shape[1]
        left[k, :channels] = jnp.concatenate([real, imag], 0).T
        left[k, channels:] = jnp.concatenate([imag, -real], 0).T
        return carry

    lax.fori_loop(0, left.shape[0], turn, 0)
    scale = 1.0 / math.sqrt(own.shape[2] * own.shape[3])
    for pair in range(rounds // 2):
        arrived(part.at[pair], part_recv.at[pair])
        if 2 * pair < AHEAD:
            def multiply(q, carry, pair=pair):
                for b in range(2):
                    products(scale, left, part, done, pair, q, b, 2 * pair)
                return carry

            lax.fori_loop(0, part.shape[1], multiply, 0)

    arrived(half_c.at[:, pl.ds(0, 31)], spread_send.at[2])
    for n in range(2):
        @pl.when(c == w)
        def _():
            arrived(held_a.at[pl.ds(0, 15)], spread_send.at[n])

        @pl.when(c != w)
        def _():
            arrived(held_a.at[pl.ds(0, 16)], spread_send.at[n])

        arrived(held_a.at[pl.ds(0, 32)], ring_send.at[n])
        arrived(held_a.at[pl.ds(0, 16)], far_send.at[n])
    arrived(held_a.at[pl.ds(0, 48)], ring_send.at[2])
    arrived(sel.at[:, 0], own_send)
    arrived(stage.at[pl.ds(0, rounds * 61)], part_send)


def products(scale, left, part, out, pair, q, b, r):
    channels = left.shape[2]
    right = jnp.concatenate(
        [
            jnp.concatenate([part[pair, q, half, n, b].reshape(-1, channels) for half in range(2)], 0)
            for n in range(2)
        ],
        1,
    )
    product = jnp.dot(left[2 * q + b], right, preferred_element_type=jnp.float32) * scale
    product = product.astype(out.dtype)
    for half in range(2):
        for n in range(2):
            out[half, r + n, 2 * q + b] = product[
                half * channels : (half + 1) * channels, n * channels : (n + 1) * channels
            ]


def move(spectra, freq_idx, pairing):
    _, _, width, channels = spectra.shape
    rounds = pairing.shape[0]
    kind = spectra.dtype
    unit = (width, channels)
    return pl.pallas_call(
        move_kernel,
        out_shape=(
            pltpu.VMEM((rounds // 2, 16, 2, 2, 2, 2) + unit, kind),
            pltpu.VMEM((32, 2 * channels, channels), kind),
            pltpu.VMEM((2, AHEAD, 32, channels, channels), kind),
        ),
        in_specs=[pl.BlockSpec(memory_space=pltpu.HBM)] * 3,
        out_specs=(pl.BlockSpec(memory_space=pltpu.VMEM),) * 3,
        scratch_shapes=[
            pltpu.VMEM(spectra.shape, kind),
            pltpu.SMEM(freq_idx.shape, freq_idx.dtype),
            pltpu.SMEM(pairing.shape, pairing.dtype),
            pltpu.VMEM((2, 2, 32) + unit, kind),
            pltpu.VMEM((2, 32, 2) + unit, kind),
            pltpu.VMEM((64, 2) + unit, kind),
            pltpu.VMEM((64, 2) + unit, kind),
            pltpu.VMEM((2, 32) + unit, kind),
            pltpu.VMEM((2, 64) + unit, kind),
            pltpu.VMEM((rounds * 64, 2) + unit, kind),
            pltpu.SemaphoreType.DMA((3,)),
            pltpu.SemaphoreType.DMA((3,)),
            pltpu.SemaphoreType.DMA((3,)),
            pltpu.SemaphoreType.DMA((3,)),
            pltpu.SemaphoreType.DMA((5,)),
            pltpu.SemaphoreType.DMA((2,)),
            pltpu.SemaphoreType.DMA((2,)),
            pltpu.SemaphoreType.DMA,
            pltpu.SemaphoreType.DMA,
            pltpu.SemaphoreType.DMA,
            pltpu.SemaphoreType.DMA((rounds // 2,)),
        ],
        compiler_params=pltpu.CompilerParams(
            collective_id=0, has_side_effects=True, vmem_limit_bytes=40 << 20
        ),
        name="move",
    )(*(pltpu.with_memory_space_constraint(a, pltpu.HBM) for a in (spectra, freq_idx, pairing)))


def finish_kernel(scale, part, left, done, out, rest, sems):
    ahead, last = done.shape[1], rest.shape[1]
    copies = []
    for half in range(2):
        for r in range(ahead):
            copies.append(pltpu.make_async_copy(done.at[half, r], out.at[half, r], sems.at[half, r]))
            copies[-1].start()
    for r in range(0, last, 2):
        def multiply(q, carry, r=r):
            for b in range(2):
                products(scale, left, part, rest, (ahead + r) // 2, q, b, r)
            return carry

        lax.fori_loop(0, part.shape[1], multiply, 0)
        for half in range(2):
            for n in (r, r + 1):
                copies.append(
                    pltpu.make_async_copy(rest.at[half, n], out.at[half, ahead + n], sems.at[half, ahead + n])
                )
                copies[-1].start()
    for copy in copies:
        copy.wait()


def finish(scale, part, left, done):
    rounds = 2 * part.shape[0]
    _, ahead, bins, channels, _ = done.shape
    return pl.pallas_call(
        functools.partial(finish_kernel, scale),
        out_shape=jax.ShapeDtypeStruct((2, rounds, bins, channels, channels), done.dtype),
        in_specs=[pl.BlockSpec(memory_space=pltpu.VMEM)] * 3,
        out_specs=pl.BlockSpec(memory_space=pltpu.HBM),
        scratch_shapes=[
            pltpu.VMEM((2, rounds - ahead, bins, channels, channels), done.dtype),
            pltpu.SemaphoreType.DMA((2, rounds)),
        ],
        compiler_params=pltpu.CompilerParams(vmem_limit_bytes=16 << 20),
        name="finish",
    )(part, left, done)


def body(spectra, freq_idx, pairing):
    scale = 1.0 / math.sqrt(spectra.shape[2] * lax.axis_size("win"))
    part, left, done = move(spectra, freq_idx, pairing)
    return finish(scale, part, left, done)


def solution(mesh):
    return jax.shard_map(
        body,
        mesh=mesh,
        in_specs=(P(None, None, "win", "chan"), P(), P()),
        out_specs=P(None, None, "win", "chan", None),
        check_vma=False,
    )
```

time: 105 us -> 93.9 us (0.89)
  Pallas kernels: 102 us -> 93.8 us
  local copies, waits for them, and re-layouts: 3.53 us -> 0 us
    pallas_call x2, Pallas kernels: 102 us -> 93.8 us  [the longest x1 88.3 us: move(): pl.pallas_call(move_kernel, out_shape=(pltpu.VMEM((rounds // 2, 16, 2, 2,...]
    unnamed x6 -> x0, local copies, waits for them, and re-layouts: 3.53 us -> none
where the time goes in v3:
time: 93.9 us; the launch traced here: 93.8 us
  Pallas kernels  93.8 us (100%)
    pallas_call x1, Pallas kernels, move(): pl.pallas_call(move_kernel, out_shape=(pltpu.VMEM((rounds // 2, 16, 2, 2,...  88.3 us
    pallas_call x1, Pallas kernels, finish(): pl.pallas_call(functools.partial(finish_kernel, scale), out_shape=jax.Sha...  5.49 us

profile of v3, /device:TPU:1, one launch (start us, length us, event | category | flops | bytes accessed | tf_op | source)
XLA Modules:
  0.0 93.8 jit_solution(987560676529161907)
XLA Ops:
  0.0 88.3 %move.1 = (bf16[3,16,2,2,2,2,32,128]{7,6,5,4,3,2,1,0:T(8,128)(2,1)S(1)}, bf16[32,256,128]{2,1,0:T(8,128)(2,1)S(1)}, bf16[2,4,32,128,128]{4,3,2,1,0:T(8,128)(2,1)S(1)}) custom-call(bf16[2,256,32,128]{3,2,1,0:T(8,128)(2,1)} %spectra.1, s32[64]{0:T(128)} %freq_in.1, s32[6,64]{1,0:T(8,128)} %pairing_in.1), custom_call_target="tpu_custom_call" | custom-call | tf_op jit(solution)/shard_map/move/pallas_call | solution.py:297
  88.3 5.5 %finish.1 = bf16[2,6,32,128,128]{4,3,2,1,0:T(8,128)(2,1)} custom-call(bf16[3,16,2,2,2,2,32,128]{7,6,5,4,3,2,1,0:T(8,128)(2,1)S(1)} %get-tuple-element.8.part, bf16[32,256,128]{2,1,0:T(8,128)(2,1)S(1)} %get-tuple-element.9.left, bf16[2,4,32,128,128]{4,3,2,1,0:T(8,128)(2,1)S(1)} %get-tuple-element.10.done), custom_call_target="tpu_custom_call" | custom-call | tf_op jit(solution)/shard_map/finish/pallas_call | solution.py:363

commit v4 on v3

v4 whole, which is shorter than its diff:
```python
import functools
import math

import jax
import jax.numpy as jnp
from jax import lax
from jax.experimental import pallas as pl
from jax.experimental.pallas import tpu as pltpu
from jax.sharding import PartitionSpec as P

MESH = pl.DeviceIdType.MESH


def block_of(x, zh, y, c):
    return ((x * 2 + zh) * 4 + y) * 2 + c


def place(x, zh, w, y, c):
    return {"chan": block_of(x, zh, y, c), "win": w}


AHEAD = 4
PIECES = 4
SIDE_BINS = 4
DEEP_BINS = 4
SIDE = ((0, 1), (1, 3))
DEEP = ((0, 1), (1, 3))


def move_kernel(
    spectra, freq_in, pairing_in, part, left, done,
    whole, freq, pairing, sel, own,
    held_a0, held_a1, held_b0, held_b1, half_c0, half_c1, held_c0, held_c1,
    stage_a0, stage_a1, stage_b0, stage_b1, stage_c0, stage_c1,
    load_sem, spread_send, spread_recv, ring_send, ring_recv, near_send, near_recv,
    far_send, far_recv, own_send, own_recv, part_send, part_recv,
):
    held_a, held_b, half_c, held_c = (held_a0, held_a1), (held_b0, held_b1), (half_c0, half_c1), (held_c0, held_c1)
    stage_a, stage_b, stage_c = (stage_a0, stage_a1), (stage_b0, stage_b1), (stage_c0, stage_c1)
    chan = lax.axis_index("chan")
    w = lax.axis_index("win")
    c = chan % 2
    y = (chan // 2) % 4
    zh = (chan // 8) % 2
    x = chan // 16
    pairs = pairing.shape[0] // 2
    first_b, first_c = 2 * SIDE_BINS, 4 * SIDE_BINS

    loads = [
        pltpu.make_async_copy(src, dst, load_sem.at[n])
        for n, (src, dst) in enumerate(((spectra, whole), (freq_in, freq), (pairing_in, pairing)))
    ]
    for load in loads:
        load.start()

    barrier = pltpu.get_barrier_semaphore()

    def greet(dx, dz, dy, dc):
        z = (zh * 2 + w + dz) % 4
        pl.semaphore_signal(
            barrier, inc=1, device_id=place((x + dx) % 4, z // 2, z % 2, (y + dy) % 4, (c + dc) % 2),
            device_id_type=MESH,
        )

    def greet_plane(o, carry):
        dc, one, two = o % 2, (o // 2) % 4, o // 8
        greet(0, one, two, dc)

        @pl.when(two > 0)
        def _():
            greet(two, one, 0, dc)

        @pl.when((one > 0) & (two > 0))
        def _():
            greet(one, 0, two, dc)

        return carry

    lax.fori_loop(1, 32, greet_plane, 0)
    for load in loads:
        load.wait()

    def pick(k, carry):
        f = freq[k]
        for half in range(2):
            sel[half, k // 32, k % 32] = whole[half, f]
        return carry

    lax.fori_loop(0, 64, pick, 0)
    pl.semaphore_wait(barrier, 31 + 24 + 18)

    def send(src, dst, ssem, rsem, target):
        pltpu.make_async_remote_copy(
            src_ref=src, dst_ref=dst, send_sem=ssem, recv_sem=rsem, device_id=target, device_id_type=MESH
        ).start()

    def arrived(ref, sem):
        pltpu.make_async_copy(ref, ref, sem).wait()

    mine_a = block_of(x, zh, y, c)
    mine_b = y * 16 + (x * 2 + zh) * 2 + c
    mine_c = (x * 4 + y) * 2 + c

    def src_a(t, zh2, w2, y2):
        start, size = SIDE[t]
        return sel.at[y2 // 2, w2, pl.ds(SIDE_BINS * (y2 % 2) + start, size), zh2]

    def src_b(t, zh2, w2, x2):
        start, size = SIDE[t]
        return sel.at[x2 // 2, w2, pl.ds(first_b + SIDE_BINS * (x2 % 2) + start, size), zh2]

    def src_c(t, x2, y2):
        start, size = DEEP[t]
        return sel.at[x2 // 2, :, pl.ds(first_c + DEEP_BINS * y2 + start, size), x2 % 2]

    def spread_a(t, o):
        zh2, w2, y2 = (zh + o) % 2, (w + o // 2) % 2, (y + o // 4) % 4
        send(
            src_a(t, zh2, w2, y2), held_a[t].at[mine_a],
            spread_send.at[t, 0], spread_recv.at[t, 0], place(x, zh2, w2, y2, w),
        )

    def spread_b(t, o):
        zh2, w2, x2 = (zh + o) % 2, (w + o // 2) % 2, (x + o // 4) % 4
        send(
            src_b(t, zh2, w2, x2), held_b[t].at[mine_b],
            spread_send.at[t, 1], spread_recv.at[t, 1], place(x2, zh2, w2, y, w),
        )

    def spread_c(t, o):
        x2, y2 = (x + o // 4) % 4, (y + o) % 4
        send(
            src_c(t, x2, y2), half_c[t].at[:, mine_c],
            spread_send.at[t, 2], spread_recv.at[t, 2], place(x2, zh, w, y2, w),
        )

    for t in range(2):
        def spread(i, carry, t=t):
            spread_c(t, (i * 5) % 16)
            spread_a(t, (i * 5) % 16)
            spread_b(t, (i * 7) % 16)
            return carry

        lax.fori_loop(1, 16, spread, 0)

        @pl.when(c == w)
        def _():
            pltpu.make_async_copy(src_a(t, zh, w, y), held_a[t].at[mine_a], spread_recv.at[t, 0]).start()
            pltpu.make_async_copy(src_b(t, zh, w, x), held_b[t].at[mine_b], spread_recv.at[t, 1]).start()
            pltpu.make_async_copy(src_c(t, x, y), half_c[t].at[:, mine_c], spread_recv.at[t, 2]).start()

        @pl.when(c != w)
        def _():
            spread_c(t, 0)
            spread_a(t, 0)
            spread_b(t, 0)

    def at_a(d):
        return place((x + d) % 4, zh, w, y, c)

    def at_b(d):
        return place(x, zh, w, (y + d) % 4, c)

    groups = ((held_a, x, at_a), (held_b, y, at_b))

    def pass_on(t):
        @pl.when(c == w)
        def _():
            arrived(half_c[t], spread_recv.at[t, 2])
            block = held_c[t].at[pl.ds(zh * 32, 32)]
            for n, (dzh, dw) in enumerate(((1, 0), (0, 1), (1, 1))):
                zh2, w2 = (zh + dzh) % 2, (w + dw) % 2
                send(half_c[t].at[w2], block, near_send.at[t, n], near_recv.at[t], place(x, zh2, w2, y, c))
            pltpu.make_async_copy(half_c[t].at[w], block, near_recv.at[t]).start()

        for n, (held, at, target) in enumerate(groups):
            block = held[t].at[pl.ds(at * 16, 16)]
            arrived(block, spread_recv.at[t, n])
            for k, d in enumerate((1, 3)):
                send(block, block, ring_send.at[t, n], ring_recv.at[t, n, k], target(d))

    def pass_far(t):
        for n, (held, at, target) in enumerate(groups):
            for k, d in enumerate((3, 1)):
                arrived(held[t].at[pl.ds(((at + d) % 4) * 16, 16)], ring_recv.at[t, n, k])
                half = held[t].at[pl.ds(((at + d) % 4) * 16 + 8 * k, 8)]
                send(half, half, far_send.at[t, n], far_recv.at[t, n], target(4 - d))

    def pass_end(t):
        for n, (held, at, target) in enumerate(groups):
            arrived(held[t].at[pl.ds(0, 16)], far_recv.at[t, n])
        arrived(held_c[t], near_recv.at[t])

    def fill_a(t, slot, pair, b):
        start, size = SIDE[t]
        for n in range(2):
            stage_a[t][slot, :, n] = held_a[t][pairing[2 * pair + n, b]]
        return part.at[pair, pl.ds(SIDE_BINS * (y % 2) + start, size), y // 2, :, c, zh]

    def fill_b(t, slot, pair, b):
        start, size = SIDE[t]
        for n in range(2):
            p = pairing[2 * pair + n, b]
            stage_b[t][slot, :, n] = held_b[t][((p // 2) % 4) * 16 + (p // 8) * 2 + p % 2]
        return part.at[pair, pl.ds(first_b + SIDE_BINS * (x % 2) + start, size), x // 2, :, c, zh]

    def fill_c(t, slot, pair, b):
        start, size = DEEP[t]
        for n in range(2):
            p = pairing[2 * pair + n, b]
            stage_c[t][slot, :, n] = held_c[t][((p // 8) % 2) * 32 + (p // 16) * 8 + p % 8]
        return part.at[pair, pl.ds(first_c + DEEP_BINS * y + start, size), x // 2, :, c, x % 2]

    def give_a(t, j):
        pair, o = j // 15, ((j % 15 + 1) * 5) % 16
        zh2, y2, c2 = (zh + o) % 2, (y + o // 2) % 4, (c + o // 8) % 2
        dst = fill_a(t, j, pair, block_of(x, zh2, y2, c2))
        send(stage_a[t].at[j], dst, part_send.at[t, 0], part_recv.at[pair], place(x, zh2, w, y2, c2))

    def give_b(t, j):
        pair, o = j // 15, ((j % 15 + 1) * 7) % 16
        zh2, x2, c2 = (zh + o) % 2, (x + o // 2) % 4, (c + o // 8) % 2
        dst = fill_b(t, j, pair, block_of(x2, zh2, y, c2))
        send(stage_b[t].at[j], dst, part_send.at[t, 1], part_recv.at[pair], place(x2, zh2, w, y, c2))

    def give_c(t, j):
        pair, o = j // 31, ((j % 31 + 1) * 5) % 32
        x2, y2, c2 = (x + o // 8) % 4, (y + o // 2) % 4, (c + o) % 2
        dst = fill_c(t, j, pair, block_of(x2, zh, y2, c2))
        send(stage_c[t].at[j], dst, part_send.at[t, 2], part_recv.at[pair], place(x2, zh, w, y2, c2))

    def give(t, begin, end):
        def step(i, carry):
            for n in range(3):
                give_c(t, pairs + 6 * i + 2 * n)
                give_a(t, 3 * i + n)
                give_c(t, pairs + 6 * i + 2 * n + 1)
                give_b(t, 3 * i + n)
            return carry

        lax.fori_loop(begin, end, step, 0)

    def keep(t):
        def step(pair, carry):
            for stage, fill, others in (
                (stage_a, fill_a, 15), (stage_b, fill_b, 15), (stage_c, fill_c, 31)
            ):
                slot = others * pairs + pair
                dst = fill(t, slot, pair, chan)
                pltpu.make_async_copy(stage[t].at[slot], dst, part_recv.at[pair]).start()
            give_c(t, pair)
            return carry

        lax.fori_loop(0, pairs, step, 0)

    turns = 5 * pairs
    pass_on(0)
    pass_far(0)
    pass_on(1)
    pass_end(0)
    keep(0)
    give(0, 0, turns // 2)
    pass_far(1)
    send(sel.at[:, 1 - w], own.at[:, :, w], own_send, own_recv, place(x, zh, 1 - w, y, c))
    pltpu.make_async_copy(sel.at[:, w], own.at[:, :, w], own_recv).start()
    give(0, turns // 2, turns)
    pass_end(1)
    keep(1)
    give(1, 0, turns)

    arrived(sel, own_recv)

    def turn(k, carry):
        real = own[0, k].reshape(-1, own.shape[-1])
        imag = own[1, k].reshape(-1, own.shape[-1])
        channels = real.shape[1]
        left[k, :channels] = jnp.concatenate([real, imag], 0).T
        left[k, channels:] = jnp.concatenate([imag, -real], 0).T
        return carry

    lax.fori_loop(0, left.shape[0], turn, 0)
    scale = 1.0 / math.sqrt(own.shape[2] * own.shape[3] * own.shape[4])
    for pair in range(pairs):
        arrived(part.at[pair], part_recv.at[pair])
        if 2 * pair < AHEAD:
            def multiply(q, carry, pair=pair):
                for b in range(2):
                    products(scale, left, part, done, pair, q, b, 2 * pair)
                return carry

            lax.fori_loop(0, part.shape[1] // 2, multiply, 0)

    for t in range(2):
        def gone(others, t=t):
            arrived(held_a[t].at[pl.ds(0, others)], spread_send.at[t, 0])
            arrived(held_b[t].at[pl.ds(0, others)], spread_send.at[t, 1])
            arrived(half_c[t].at[:, pl.ds(0, others)], spread_send.at[t, 2])

        @pl.when(c == w)
        def _():
            gone(15)
            for n in range(3):
                arrived(held_c[t].at[pl.ds(0, 32)], near_send.at[t, n])

        @pl.when(c != w)
        def _():
            gone(16)

        for n in range(2):
            arrived(held_a[t].at[pl.ds(0, 32)], ring_send.at[t, n])
            arrived(held_a[t].at[pl.ds(0, 16)], far_send.at[t, n])
        for n, (stage, others) in enumerate(((stage_a, 15), (stage_b, 15), (stage_c, 31))):
            arrived(stage[t].at[pl.ds(0, others * pairs)], part_send.at[t, n])
    arrived(sel.at[:, 0], own_send)


def products(scale, left, part, out, pair, q, b, r):
    channels = left.shape[2]
    right = jnp.concatenate(
        [
            jnp.concatenate([part[pair, 2 * q + b, half, n].reshape(-1, channels) for half in range(2)], 0)
            for n in range(2)
        ],
        1,
    )
    product = jnp.dot(left[2 * q + b], right, preferred_element_type=jnp.float32) * scale
    product = product.astype(out.dtype)
    for half in range(2):
        for n in range(2):
            out[half, r + n, 2 * q + b] = product[
                half * channels : (half + 1) * channels, n * channels : (n + 1) * channels
            ]


def move(spectra, freq_idx, pairing):
    _, nbins, width, channels = spectra.shape
    rounds = pairing.shape[0]
    kind = spectra.dtype
    tile = (width // 2, channels)
    spectra = spectra.reshape((2, nbins, 2) + tile)
    side, deep = [n for _, n in SIDE], [n for _, n in DEEP]
    return pl.pallas_call(
        move_kernel,
        out_shape=(
            pltpu.VMEM((rounds // 2, 32, 2, 2, 2, 2) + tile, kind),
            pltpu.VMEM((32, 2 * channels, channels), kind),
            pltpu.VMEM((2, AHEAD, 32, channels, channels), kind),
        ),
        in_specs=[pl.BlockSpec(memory_space=pltpu.HBM)] * 3,
        out_specs=(pl.BlockSpec(memory_space=pltpu.VMEM),) * 3,
        scratch_shapes=[
            pltpu.VMEM(spectra.shape, kind),
            pltpu.SMEM(freq_idx.shape, freq_idx.dtype),
            pltpu.SMEM(pairing.shape, pairing.dtype),
            pltpu.VMEM((2, 2, 32, 2) + tile, kind),
            pltpu.VMEM((2, 32, 2, 2) + tile, kind),
            *[pltpu.VMEM((64, n) + tile, kind) for n in side],
            *[pltpu.VMEM((64, n) + tile, kind) for n in side],
            *[pltpu.VMEM((2, 32, n) + tile, kind) for n in deep],
            *[pltpu.VMEM((64, n) + tile, kind) for n in deep],
            *[pltpu.VMEM((8 * rounds, n, 2) + tile, kind) for n in side],
            *[pltpu.VMEM((8 * rounds, n, 2) + tile, kind) for n in side],
            *[pltpu.VMEM((16 * rounds, n, 2) + tile, kind) for n in deep],
            pltpu.SemaphoreType.DMA((3,)),
            pltpu.SemaphoreType.DMA((2, 3)),
            pltpu.SemaphoreType.DMA((2, 3)),
            pltpu.SemaphoreType.DMA((2, 2)),
            pltpu.SemaphoreType.DMA((2, 2, 2)),
            pltpu.SemaphoreType.DMA((2, 3)),
            pltpu.SemaphoreType.DMA((2,)),
            pltpu.SemaphoreType.DMA((2, 2)),
            pltpu.SemaphoreType.DMA((2, 2)),
            pltpu.SemaphoreType.DMA,
            pltpu.SemaphoreType.DMA,
            pltpu.SemaphoreType.DMA((2, 3)),
            pltpu.SemaphoreType.DMA((rounds // 2,)),
        ],
        compiler_params=pltpu.CompilerParams(
            collective_id=0, has_side_effects=True, vmem_limit_bytes=40 << 20
        ),
        name="move",
    )(*(pltpu.with_memory_space_constraint(a, pltpu.HBM) for a in (spectra, freq_idx, pairing)))


def finish_kernel(scale, part, left, done, out, rest, sems, rest_sems):
    ahead, last = done.shape[1], rest.shape[1]
    copies = []
    for half in range(2):
        for r in range(ahead):
            copies.append(pltpu.make_async_copy(done.at[half, r], out.at[half, r], sems.at[half, r]))
            copies[-1].start()
    groups = part.shape[1] // 2
    for r in range(0, last, 2):
        for piece in range(PIECES):
            def multiply(q, carry, r=r):
                for b in range(2):
                    products(scale, left, part, rest, (ahead + r) // 2, q, b, r)
                return carry

            size = groups // PIECES
            lax.fori_loop(piece * size, (piece + 1) * size, multiply, 0)
            bins = pl.ds(piece * size * 2, size * 2)
            for half in range(2):
                copies.append(
                    pltpu.make_async_copy(
                        rest.at[half, pl.ds(r, 2), bins],
                        out.at[half, pl.ds(ahead + r, 2), bins],
                        rest_sems.at[r // 2, half, piece],
                    )
                )
                copies[-1].start()
    for copy in copies:
        copy.wait()


def finish(scale, part, left, done):
    rounds = 2 * part.shape[0]
    _, ahead, bins, channels, _ = done.shape
    return pl.pallas_call(
        functools.partial(finish_kernel, scale),
        out_shape=jax.ShapeDtypeStruct((2, rounds, bins, channels, channels), done.dtype),
        in_specs=[pl.BlockSpec(memory_space=pltpu.VMEM)] * 3,
        out_specs=pl.BlockSpec(memory_space=pltpu.HBM),
        scratch_shapes=[
            pltpu.VMEM((2, rounds - ahead, bins, channels, channels), done.dtype),
            pltpu.SemaphoreType.DMA((2, ahead)),
            pltpu.SemaphoreType.DMA(((rounds - ahead) // 2, 2, PIECES)),
        ],
        compiler_params=pltpu.CompilerParams(vmem_limit_bytes=16 << 20),
        name="finish",
    )(part, left, done)


def body(spectra, freq_idx, pairing):
    scale = 1.0 / math.sqrt(spectra.shape[2] * lax.axis_size("win"))
    part, left, done = move(spectra, freq_idx, pairing)
    return finish(scale, part, left, done)


def solution(mesh):
    return jax.shard_map(
        body,
        mesh=mesh,
        in_specs=(P(None, None, "win", "chan"), P(), P()),
        out_specs=P(None, None, "win", "chan", None),
        check_vma=False,
    )
```

time: 93.9 us -> 88.1 us (0.938)
  Pallas kernels: 93.8 us -> 87.9 us
    pallas_call x1, Pallas kernels: 88.3 us -> 83.3 us  [move(): pl.pallas_call(move_kernel, out_shape=(pltpu.VMEM((rounds // 2, 32, 2, 2,...]
where the time goes in v4:
time: 88.1 us; the launch traced here: 88 us
  Pallas kernels  87.9 us (100%)
    pallas_call x1, Pallas kernels, move(): pl.pallas_call(move_kernel, out_shape=(pltpu.VMEM((rounds // 2, 32, 2, 2,...  83.3 us
    pallas_call x1, Pallas kernels, finish(): pl.pallas_call(functools.partial(finish_kernel, scale), out_shape=jax.Sha...  4.68 us

profile of v4, /device:TPU:1, one launch (start us, length us, event | category | flops | bytes accessed | tf_op | source)
XLA Modules:
  0.0 88.0 jit_solution(5173330081910543755)
XLA Ops:
  0.0 83.3 %move.1 = (bf16[3,32,2,2,2,2,16,128]{7,6,5,4,3,2,1,0:T(8,128)(2,1)S(1)}, bf16[32,256,128]{2,1,0:T(8,128)(2,1)S(1)}, bf16[2,4,32,128,128]{4,3,2,1,0:T(8,128)(2,1)S(1)}) custom-call(bf16[2,256,2,16,128]{4,3,2,1,0:T(8,128)(2,1)} %bitcast.1, s32[64]{0:T(128)} %freq_in.1, s32[6,64]{1,0:T(8,128)} %pairing_in.1), custom_call_target="tpu_custom_call" | custom-call | tf_op jit(solution)/shard_map/move/pallas_call | solution.py:342
  83.3 4.7 %finish.1 = bf16[2,6,32,128,128]{4,3,2,1,0:T(8,128)(2,1)} custom-call(bf16[3,32,2,2,2,2,16,128]{7,6,5,4,3,2,1,0:T(8,128)(2,1)S(1)} %get-tuple-element.8.part, bf16[32,256,128]{2,1,0:T(8,128)(2,1)S(1)} %get-tuple-element.9.left, bf16[2,4,32,128,128]{4,3,2,1,0:T(8,128)(2,1)S(1)} %get-tuple-element.10.done), custom_call_target="tpu_custom_call" | custom-call | tf_op jit(solution)/shard_map/finish/pallas_call | solution.py:419

commit v5 on v4

v5 whole, which is shorter than its diff:
```python
import functools
import math

import jax
import jax.numpy as jnp
from jax import lax
from jax.experimental import pallas as pl
from jax.experimental.pallas import tpu as pltpu
from jax.sharding import PartitionSpec as P

MESH = pl.DeviceIdType.MESH


def block_of(x, zh, y, c):
    return ((x * 2 + zh) * 4 + y) * 2 + c


def place(x, zh, w, y, c):
    return {"chan": block_of(x, zh, y, c), "win": w}


AHEAD = 4
PIECES = 4
BINS = 4
CUTS = ((0, 1), (1, 3))


def move_kernel(
    spectra, freq_in, pairing_in, part, left, done,
    whole, freq, pairing, sel, own,
    held_a0, held_a1, held_b0, held_b1, held_c0, held_c1, held_d0, held_d1,
    half_c0, half_c1, half_d0, half_d1,
    stage_a0, stage_a1, stage_b0, stage_b1, stage_c0, stage_c1, stage_d0, stage_d1,
    load_sem, spread_send, spread_recv, ring_send, ring_recv, far_send, far_recv, near_send, near_recv,
    mate_send, mate_recv, own_send, own_recv, part_send, part_recv,
):
    held = ((held_a0, held_a1), (held_b0, held_b1), (held_c0, held_c1), (held_d0, held_d1))
    half = ((half_c0, half_c1), (half_d0, half_d1))
    stage = ((stage_a0, stage_a1), (stage_b0, stage_b1), (stage_c0, stage_c1), (stage_d0, stage_d1))
    chan = lax.axis_index("chan")
    w = lax.axis_index("win")
    c = chan % 2
    y = (chan // 2) % 4
    zh = (chan // 8) % 2
    x = chan // 16
    pairs = pairing.shape[0] // 2

    loads = [
        pltpu.make_async_copy(src, dst, load_sem.at[n])
        for n, (src, dst) in enumerate(((spectra, whole), (freq_in, freq), (pairing_in, pairing)))
    ]
    for load in loads:
        load.start()

    barrier = pltpu.get_barrier_semaphore()

    def greet(dx, dz, dy, dc):
        z = (zh * 2 + w + dz) % 4
        pl.semaphore_signal(
            barrier, inc=1, device_id=place((x + dx) % 4, z // 2, z % 2, (y + dy) % 4, (c + dc) % 2),
            device_id_type=MESH,
        )

    def greet_plane(o, carry):
        dc, one, two = o % 2, (o // 2) % 4, o // 8
        greet(0, one, two, dc)

        @pl.when(two > 0)
        def _():
            greet(two, one, 0, dc)

        @pl.when((one > 0) & (two > 0))
        def _():
            greet(one, 0, two, dc)

        return carry

    lax.fori_loop(1, 32, greet_plane, 0)
    for load in loads:
        load.wait()

    def pick(k, carry):
        f = freq[k]
        for half in range(2):
            sel[half, k // 32, k % 32] = whole[half, f]
        return carry

    lax.fori_loop(0, 64, pick, 0, unroll=8)
    pl.semaphore_wait(barrier, 31 + 24 + 18)

    def send(src, dst, ssem, rsem, target):
        pltpu.make_async_remote_copy(
            src_ref=src, dst_ref=dst, send_sem=ssem, recv_sem=rsem, device_id=target, device_id_type=MESH
        ).start()

    def arrived(ref, sem):
        pltpu.make_async_copy(ref, ref, sem).wait()

    def bins_of(n, t, group):
        start, size = CUTS[t]
        return pl.ds((2 * n + group) * BINS + start, size)

    def chunk_of(n, zh2, x2, y2, core):
        major = y2 if n in (0, 2) else x2
        minor = (zh2, zh2, pair_of(x2, core), pair_of(y2, core))[n]
        return major % 2, major // 2, minor

    def pick_by(core, zero, one):
        return (1 - core) * zero + core * one

    def across(at, bit, core):
        return at + bit * pick_by(core, 3 - 2 * at, 1 - 2 * (at % 2))

    def pair_of(at, core):
        return pick_by(core, at // 2, ((at + 1) // 2) % 2)

    def side_of(at, core):
        return pair_of(at, 1 - core)

    def index_of(n, p):
        x2, zh2, y2, c2 = p // 16, (p // 8) % 2, (p // 2) % 4, p % 2
        if n == 0:
            return p
        if n == 1:
            return y2 * 16 + x2 * 4 + zh2 * 2 + c2
        if n == 2:
            return side_of(x2, c) * 32 + zh2 * 16 + pair_of(x2, c) * 8 + y2 * 2 + c2
        return side_of(y2, c) * 32 + zh2 * 16 + pair_of(y2, c) * 8 + x2 * 2 + c2

    mine_half = (pair_of(x, w) * 8 + y * 2 + c, pair_of(y, w) * 8 + x * 2 + c)

    def source(n, t, zh2, w2, x2, y2):
        group, part_half, windows = chunk_of(n, zh2, x2, y2, w)
        return sel.at[part_half, w2 if n < 2 else slice(None), bins_of(n, t, group), windows]

    def landing(n, t):
        return held[n][t].at[index_of(n, chan)] if n < 2 else half[n - 2][t].at[:, mine_half[n - 2]]

    def spread_to(n, o):
        if n == 0:
            return (zh + o) % 2, (w + o // 2) % 2, x, (y + o // 4) % 4
        if n == 1:
            return (zh + o) % 2, (w + o // 2) % 2, (x + o // 4) % 4, y
        if n == 2:
            return zh, w, across(x, o % 2, w), (y + o // 2) % 4
        return zh, w, (x + o // 2) % 4, across(y, o % 2, w)

    def spread_one(n, t, o):
        zh2, w2, x2, y2 = spread_to(n, o)
        send(
            source(n, t, zh2, w2, x2, y2), landing(n, t),
            spread_send.at[t, n], spread_recv.at[t, n], place(x2, zh2, w2, y2, w),
        )

    for t in range(2):
        def spread(i, carry, t=t):
            spread_one(2, t, (i * 3) % 8)
            spread_one(0, t, (i * 10) % 16)
            spread_one(1, t, (i * 14) % 16)
            spread_one(3, t, (i * 5) % 8)
            spread_one(0, t, (i * 10 + 5) % 16)
            spread_one(1, t, (i * 14 + 7) % 16)
            return carry

        lax.fori_loop(1, 8, spread, 0)
        spread_one(0, t, 5)
        spread_one(1, t, 7)

        @pl.when(c == w)
        def _():
            for n in range(4):
                pltpu.make_async_copy(source(n, t, zh, w, x, y), landing(n, t), spread_recv.at[t, n]).start()

        @pl.when(c != w)
        def _():
            for n in range(4):
                spread_one(n, t, 0)

    def line(n, d):
        return place((x + d) % 4, zh, w, y, c) if n == 0 else place(x, zh, w, (y + d) % 4, c)

    sides = (side_of(x, c), side_of(y, c))
    mates = (place(across(x, 1, 1 - c), zh, w, y, c), place(x, zh, w, across(y, 1, 1 - c), c))

    def pass_on(t):
        @pl.when(c == w)
        def _():
            for n in range(2):
                arrived(half[n][t], spread_recv.at[t, 2 + n])
                block = held[2 + n][t].at[pl.ds(sides[n] * 32 + zh * 16, 16)]
                for k, (dzh, dw) in enumerate(((1, 0), (0, 1), (1, 1))):
                    zh2, w2 = (zh + dzh) % 2, (w + dw) % 2
                    send(half[n][t].at[w2], block, near_send.at[t, n, k], near_recv.at[t, n], place(x, zh2, w2, y, c))
                pltpu.make_async_copy(half[n][t].at[w], block, near_recv.at[t, n]).start()

        for n, at in enumerate((x, y)):
            block = held[n][t].at[pl.ds(at * 16, 16)]
            arrived(block, spread_recv.at[t, n])
            for k, d in enumerate((1, 3)):
                send(block, block, ring_send.at[t, n], ring_recv.at[t, n, k], line(n, d))

    def pass_far(t):
        for n, at in enumerate((x, y)):
            for k, d in enumerate((3, 1)):
                arrived(held[n][t].at[pl.ds(((at + d) % 4) * 16, 16)], ring_recv.at[t, n, k])
                block = held[n][t].at[pl.ds(((at + d) % 4) * 16 + 8 * k, 8)]
                send(block, block, far_send.at[t, n], far_recv.at[t, n], line(n, 4 - d))
        for n in range(2):
            block = held[2 + n][t].at[pl.ds(sides[n] * 32, 32)]
            arrived(block, near_recv.at[t, n])
            send(block, block, mate_send.at[t, n], mate_recv.at[t, n], mates[n])

    def pass_end(t):
        for n in range(2):
            arrived(held[n][t].at[pl.ds(0, 16)], far_recv.at[t, n])
            arrived(held[2 + n][t].at[pl.ds(0, 32)], mate_recv.at[t, n])

    def fill(n, t, slot, pair, b):
        for k in range(2):
            stage[n][t][slot, :, k] = held[n][t][index_of(n, pairing[2 * pair + k, b])]
        group, part_half, windows = chunk_of(n, zh, x, y, c)
        return part.at[pair, bins_of(n, t, group), part_half, :, c, windows]

    def give_one(n, t, j):
        pair, o = j // 15, ((j % 15 + 1) * (5, 7, 11, 13)[n]) % 16
        c2 = (c + o // 8) % 2
        zh2, x2, y2 = (
            ((zh + o) % 2, x, (y + o // 2) % 4),
            ((zh + o // 4) % 2, (x + o) % 4, y),
            (zh, across(x, (o // 4) % 2, c), (y + o) % 4),
            (zh, (x + o // 2) % 4, across(y, o % 2, c)),
        )[n]
        dst = fill(n, t, j, pair, block_of(x2, zh2, y2, c2))
        send(stage[n][t].at[j], dst, part_send.at[t, n], part_recv.at[pair], place(x2, zh2, w, y2, c2))

    def give(t, begin, end):
        def step(i, carry):
            for k in range(3):
                for n in (0, 2, 1, 3):
                    give_one(n, t, 3 * i + k)
            return carry

        lax.fori_loop(begin, end, step, 0)

    def keep(t):
        def step(pair, carry):
            for n in range(4):
                slot = 15 * pairs + pair
                dst = fill(n, t, slot, pair, chan)
                pltpu.make_async_copy(stage[n][t].at[slot], dst, part_recv.at[pair]).start()
            return carry

        lax.fori_loop(0, pairs, step, 0)

    turns = 5 * pairs
    pass_on(0)
    pass_far(0)
    pass_on(1)
    pass_end(0)
    keep(0)
    give(0, 0, turns // 5)
    pass_far(1)
    send(sel.at[:, 1 - w], own.at[:, :, w], own_send, own_recv, place(x, zh, 1 - w, y, c))
    pltpu.make_async_copy(sel.at[:, w], own.at[:, :, w], own_recv).start()
    give(0, turns // 5, turns)
    pass_end(1)
    keep(1)
    give(1, 0, turns)

    arrived(sel, own_recv)

    def turn(k, carry):
        real = own[0, k].reshape(-1, own.shape[-1])
        imag = own[1, k].reshape(-1, own.shape[-1])
        channels = real.shape[1]
        left[k, :channels] = jnp.concatenate([real, imag], 0).T
        left[k, channels:] = jnp.concatenate([imag, -real], 0).T
        return carry

    lax.fori_loop(0, left.shape[0], turn, 0)
    scale = 1.0 / math.sqrt(own.shape[2] * own.shape[3] * own.shape[4])
    for pair in range(pairs):
        arrived(part.at[pair], part_recv.at[pair])
        if 2 * pair < AHEAD:
            def multiply(q, carry, pair=pair):
                for b in range(2):
                    products(scale, left, part, done, pair, q, b, 2 * pair)
                return carry

            lax.fori_loop(0, part.shape[1] // 2, multiply, 0)

    for t in range(2):
        def gone(missing, t=t):
            for n in range(2):
                arrived(held[n][t].at[pl.ds(0, 16 - missing)], spread_send.at[t, n])
                arrived(half[n][t].at[:, pl.ds(0, 8 - missing)], spread_send.at[t, 2 + n])

        @pl.when(c == w)
        def _():
            gone(1)
            for n in range(2):
                for k in range(3):
                    arrived(held[2 + n][t].at[pl.ds(0, 16)], near_send.at[t, n, k])

        @pl.when(c != w)
        def _():
            gone(0)

        for n in range(2):
            arrived(held[n][t].at[pl.ds(0, 32)], ring_send.at[t, n])
            arrived(held[n][t].at[pl.ds(0, 16)], far_send.at[t, n])
            arrived(held[2 + n][t].at[pl.ds(0, 32)], mate_send.at[t, n])
        for n in range(4):
            arrived(stage[n][t].at[pl.ds(0, 15 * pairs)], part_send.at[t, n])
    arrived(sel.at[:, 0], own_send)


def products(scale, left, part, out, pair, q, b, r):
    channels = left.shape[2]
    right = jnp.concatenate(
        [
            jnp.concatenate([part[pair, 2 * q + b, half, n].reshape(-1, channels) for half in range(2)], 0)
            for n in range(2)
        ],
        1,
    )
    product = jnp.dot(left[2 * q + b], right, preferred_element_type=jnp.float32) * scale
    product = product.astype(out.dtype)
    for half in range(2):
        for n in range(2):
            out[half, r + n, 2 * q + b] = product[
                half * channels : (half + 1) * channels, n * channels : (n + 1) * channels
            ]


def move(spectra, freq_idx, pairing):
    _, nbins, width, channels = spectra.shape
    rounds = pairing.shape[0]
    kind = spectra.dtype
    tile = (width // 2, channels)
    spectra = spectra.reshape((2, nbins, 2) + tile)
    sizes = [n for _, n in CUTS]
    return pl.pallas_call(
        move_kernel,
        out_shape=(
            pltpu.VMEM((rounds // 2, 32, 2, 2, 2, 2) + tile, kind),
            pltpu.VMEM((32, 2 * channels, channels), kind),
            pltpu.VMEM((2, AHEAD, 32, channels, channels), kind),
        ),
        in_specs=[pl.BlockSpec(memory_space=pltpu.HBM)] * 3,
        out_specs=(pl.BlockSpec(memory_space=pltpu.VMEM),) * 3,
        scratch_shapes=[
            pltpu.VMEM(spectra.shape, kind),
            pltpu.SMEM(freq_idx.shape, freq_idx.dtype),
            pltpu.SMEM(pairing.shape, pairing.dtype),
            pltpu.VMEM((2, 2, 32, 2) + tile, kind),
            pltpu.VMEM((2, 32, 2, 2) + tile, kind),
            *[pltpu.VMEM((64, n) + tile, kind) for _ in range(4) for n in sizes],
            *[pltpu.VMEM((2, 16, n) + tile, kind) for _ in range(2) for n in sizes],
            *[pltpu.VMEM((8 * rounds, n, 2) + tile, kind) for _ in range(4) for n in sizes],
            pltpu.SemaphoreType.DMA((3,)),
            pltpu.SemaphoreType.DMA((2, 4)),
            pltpu.SemaphoreType.DMA((2, 4)),
            pltpu.SemaphoreType.DMA((2, 2)),
            pltpu.SemaphoreType.DMA((2, 2, 2)),
            pltpu.SemaphoreType.DMA((2, 2)),
            pltpu.SemaphoreType.DMA((2, 2)),
            pltpu.SemaphoreType.DMA((2, 2, 3)),
            pltpu.SemaphoreType.DMA((2, 2)),
            pltpu.SemaphoreType.DMA((2, 2)),
            pltpu.SemaphoreType.DMA((2, 2)),
            pltpu.SemaphoreType.DMA,
            pltpu.SemaphoreType.DMA,
            pltpu.SemaphoreType.DMA((2, 4)),
            pltpu.SemaphoreType.DMA((rounds // 2,)),
        ],
        compiler_params=pltpu.CompilerParams(
            collective_id=0, has_side_effects=True, vmem_limit_bytes=40 << 20
        ),
        name="move",
    )(*(pltpu.with_memory_space_constraint(a, pltpu.HBM) for a in (spectra, freq_idx, pairing)))


def finish_kernel(scale, part, left, done, out, rest, sems, rest_sems):
    ahead, last = done.shape[1], rest.shape[1]
    copies = []
    for half in range(2):
        for r in range(ahead):
            copies.append(pltpu.make_async_copy(done.at[half, r], out.at[half, r], sems.at[half, r]))
            copies[-1].start()
    groups = part.shape[1] // 2
    for r in range(0, last, 2):
        for piece in range(PIECES):
            def multiply(q, carry, r=r):
                for b in range(2):
                    products(scale, left, part, rest, (ahead + r) // 2, q, b, r)
                return carry

            size = groups // PIECES
            lax.fori_loop(piece * size, (piece + 1) * size, multiply, 0)
            bins = pl.ds(piece * size * 2, size * 2)
            for half in range(2):
                copies.append(
                    pltpu.make_async_copy(
                        rest.at[half, pl.ds(r, 2), bins],
                        out.at[half, pl.ds(ahead + r, 2), bins],
                        rest_sems.at[r // 2, half, piece],
                    )
                )
                copies[-1].start()
    for copy in copies:
        copy.wait()


def finish(scale, part, left, done):
    rounds = 2 * part.shape[0]
    _, ahead, bins, channels, _ = done.shape
    return pl.pallas_call(
        functools.partial(finish_kernel, scale),
        out_shape=jax.ShapeDtypeStruct((2, rounds, bins, channels, channels), done.dtype),
        in_specs=[pl.BlockSpec(memory_space=pltpu.VMEM)] * 3,
        out_specs=pl.BlockSpec(memory_space=pltpu.HBM),
        scratch_shapes=[
            pltpu.VMEM((2, rounds - ahead, bins, channels, channels), done.dtype),
            pltpu.SemaphoreType.DMA((2, ahead)),
            pltpu.SemaphoreType.DMA(((rounds - ahead) // 2, 2, PIECES)),
        ],
        compiler_params=pltpu.CompilerParams(vmem_limit_bytes=16 << 20),
        name="finish",
    )(part, left, done)


def body(spectra, freq_idx, pairing):
    scale = 1.0 / math.sqrt(spectra.shape[2] * lax.axis_size("win"))
    part, left, done = move(spectra, freq_idx, pairing)
    return finish(scale, part, left, done)


def solution(mesh):
    return jax.shard_map(
        body,
        mesh=mesh,
        in_specs=(P(None, None, "win", "chan"), P(), P()),
        out_specs=P(None, None, "win", "chan", None),
        check_vma=False,
    )
```

time: 88.1 us -> 86.4 us (0.981)
  Pallas kernels: 87.9 us -> 86.3 us
    pallas_call x1, Pallas kernels: 83.3 us -> 81.6 us  [move(): pl.pallas_call(move_kernel, out_shape=(pltpu.VMEM((rounds // 2, 32, 2, 2,...]
where the time goes in v5:
time: 86.4 us; the launch traced here: 86.3 us
  Pallas kernels  86.3 us (100%)
    pallas_call x1, Pallas kernels, move(): pl.pallas_call(move_kernel, out_shape=(pltpu.VMEM((rounds // 2, 32, 2, 2,...  81.6 us
    pallas_call x1, Pallas kernels, finish(): pl.pallas_call(functools.partial(finish_kernel, scale), out_shape=jax.Sha...  4.68 us

profile of v5, /device:TPU:1, one launch (start us, length us, event | category | flops | bytes accessed | tf_op | source)
XLA Modules:
  0.0 86.3 jit_solution(10045724920437110631)
XLA Ops:
  0.0 81.6 %move.1 = (bf16[3,32,2,2,2,2,16,128]{7,6,5,4,3,2,1,0:T(8,128)(2,1)S(1)}, bf16[32,256,128]{2,1,0:T(8,128)(2,1)S(1)}, bf16[2,4,32,128,128]{4,3,2,1,0:T(8,128)(2,1)S(1)}) custom-call(bf16[2,256,2,16,128]{4,3,2,1,0:T(8,128)(2,1)} %bitcast.1, s32[64]{0:T(128)} %freq_in.1, s32[6,64]{1,0:T(8,128)} %pairing_in.1), custom_call_target="tpu_custom_call" | custom-call | tf_op jit(solution)/shard_map/move/pallas_call | solution.py:343
  81.6 4.7 %finish.1 = bf16[2,6,32,128,128]{4,3,2,1,0:T(8,128)(2,1)} custom-call(bf16[3,32,2,2,2,2,16,128]{7,6,5,4,3,2,1,0:T(8,128)(2,1)S(1)} %get-tuple-element.8.part, bf16[32,256,128]{2,1,0:T(8,128)(2,1)S(1)} %get-tuple-element.9.left, bf16[2,4,32,128,128]{4,3,2,1,0:T(8,128)(2,1)S(1)} %get-tuple-element.10.done), custom_call_target="tpu_custom_call" | custom-call | tf_op jit(solution)/shard_map/finish/pallas_call | solution.py:418

commit v6 on v5

--- a/solution.py
+++ b/solution.py
@@ -27,7 +27,7 @@
 
 def move_kernel(
     spectra, freq_in, pairing_in, part, left, done,
-    whole, freq, pairing, sel, own,
+    whole_real, whole_imag, freq, pairing, sel, own,
     held_a0, held_a1, held_b0, held_b1, held_c0, held_c1, held_d0, held_d1,
     half_c0, half_c1, half_d0, half_d1,
     stage_a0, stage_a1, stage_b0, stage_b1, stage_c0, stage_c1, stage_d0, stage_d1,
@@ -47,7 +47,9 @@
 
     loads = [
         pltpu.make_async_copy(src, dst, load_sem.at[n])
-        for n, (src, dst) in enumerate(((spectra, whole), (freq_in, freq), (pairing_in, pairing)))
+        for n, (src, dst) in enumerate(
+            ((freq_in, freq), (pairing_in, pairing), (spectra.at[0], whole_real), (spectra.at[1], whole_imag))
+        )
     ]
     for load in loads:
         load.start()
@@ -76,16 +78,16 @@
         return carry
 
     lax.fori_loop(1, 32, greet_plane, 0)
-    for load in loads:
-        load.wait()
-
-    def pick(k, carry):
-        f = freq[k]
-        for half in range(2):
-            sel[half, k // 32, k % 32] = whole[half, f]
-        return carry
-
-    lax.fori_loop(0, 64, pick, 0, unroll=8)
+    loads[0].wait()
+    for half_at, whole in enumerate((whole_real, whole_imag)):
+        loads[2 + half_at].wait()
+
+        def pick(k, carry, half_at=half_at, whole=whole):
+            sel[half_at, k // 32, k % 32] = whole[freq[k]]
+            return carry
+
+        lax.fori_loop(0, 64, pick, 0, unroll=16)
+    loads[1].wait()
     pl.semaphore_wait(barrier, 31 + 24 + 18)
 
     def send(src, dst, ssem, rsem, target):
@@ -154,14 +156,18 @@
 
     for t in range(2):
         def spread(i, carry, t=t):
-            spread_one(2, t, (i * 3) % 8)
             spread_one(0, t, (i * 10) % 16)
             spread_one(1, t, (i * 14) % 16)
-            spread_one(3, t, (i * 5) % 8)
             spread_one(0, t, (i * 10 + 5) % 16)
             spread_one(1, t, (i * 14 + 7) % 16)
             return carry
 
+        def spread_deep(i, carry, t=t):
+            spread_one(2, t, (i * 3) % 8)
+            spread_one(3, t, (i * 5) % 8)
+            return carry
+
+        lax.fori_loop(1, 8, spread_deep, 0)
         lax.fori_loop(1, 8, spread, 0)
         spread_one(0, t, 5)
         spread_one(1, t, 7)
@@ -216,13 +222,21 @@
             arrived(held[2 + n][t].at[pl.ds(0, 32)], mate_recv.at[t, n])
 
     def fill(n, t, slot, pair, b):
+        group, part_half, windows = chunk_of(n, zh, x, y, c)
+        bins = bins_of(n, t, group)
+        if t == 0:
+            for r in range(2 * pairs):
+                stage[n][t][slot, r // 2, :, r % 2] = held[n][t][index_of(n, pairing[r, b])]
+            return part.at[:, bins, part_half, :, c, windows]
         for k in range(2):
             stage[n][t][slot, :, k] = held[n][t][index_of(n, pairing[2 * pair + k, b])]
-        group, part_half, windows = chunk_of(n, zh, x, y, c)
-        return part.at[pair, bins_of(n, t, group), part_half, :, c, windows]
+        return part.at[pair, bins, part_half, :, c, windows]
+
+    def due(t, pair):
+        return part_recv.at[pairs if t == 0 else pair]
 
     def give_one(n, t, j):
-        pair, o = j // 15, ((j % 15 + 1) * (5, 7, 11, 13)[n]) % 16
+        pair, o = j // 15, ((j % 15 + 1) * (5, 11, 3, 7)[n]) % 16
         c2 = (c + o // 8) % 2
         zh2, x2, y2 = (
             ((zh + o) % 2, x, (y + o // 2) % 4),
@@ -231,13 +245,14 @@
             (zh, (x + o // 2) % 4, across(y, o % 2, c)),
         )[n]
         dst = fill(n, t, j, pair, block_of(x2, zh2, y2, c2))
-        send(stage[n][t].at[j], dst, part_send.at[t, n], part_recv.at[pair], place(x2, zh2, w, y2, c2))
+        send(stage[n][t].at[j], dst, part_send.at[t, n], due(t, pair), place(x2, zh2, w, y2, c2))
 
     def give(t, begin, end):
         def step(i, carry):
-            for k in range(3):
+            each = 1 if t == 0 else pairs
+            for k in range(each):
                 for n in (0, 2, 1, 3):
-                    give_one(n, t, 3 * i + k)
+                    give_one(n, t, each * i + k)
             return carry
 
         lax.fori_loop(begin, end, step, 0)
@@ -245,14 +260,15 @@
     def keep(t):
         def step(pair, carry):
             for n in range(4):
-                slot = 15 * pairs + pair
+                slot = copies[t] + pair
                 dst = fill(n, t, slot, pair, chan)
-                pltpu.make_async_copy(stage[n][t].at[slot], dst, part_recv.at[pair]).start()
+                pltpu.make_async_copy(stage[n][t].at[slot], dst, due(t, pair)).start()
             return carry
 
-        lax.fori_loop(0, pairs, step, 0)
-
-    turns = 5 * pairs
+        lax.fori_loop(0, copies[t] // 15, step, 0)
+
+    copies = (15, 15 * pairs)
+    turns = 15
     pass_on(0)
     pass_far(0)
     pass_on(1)
@@ -279,8 +295,10 @@
 
     lax.fori_loop(0, left.shape[0], turn, 0)
     scale = 1.0 / math.sqrt(own.shape[2] * own.shape[3] * own.shape[4])
+    early = part.shape[1] * CUTS[0][1] // BINS
+    arrived(part.at[0, pl.ds(0, early * pairs)], part_recv.at[pairs])
     for pair in range(pairs):
-        arrived(part.at[pair], part_recv.at[pair])
+        arrived(part.at[pair, pl.ds(early, part.shape[1] - early)], part_recv.at[pair])
         if 2 * pair < AHEAD:
             def multiply(q, carry, pair=pair):
                 for b in range(2):
@@ -311,7 +329,7 @@
             arrived(held[n][t].at[pl.ds(0, 16)], far_send.at[t, n])
             arrived(held[2 + n][t].at[pl.ds(0, 32)], mate_send.at[t, n])
         for n in range(4):
-            arrived(stage[n][t].at[pl.ds(0, 15 * pairs)], part_send.at[t, n])
+            arrived(stage[n][t].at[pl.ds(0, copies[t])], part_send.at[t, n])
     arrived(sel.at[:, 0], own_send)
 
 
@@ -350,15 +368,20 @@
         in_specs=[pl.BlockSpec(memory_space=pltpu.HBM)] * 3,
         out_specs=(pl.BlockSpec(memory_space=pltpu.VMEM),) * 3,
         scratch_shapes=[
-            pltpu.VMEM(spectra.shape, kind),
+            pltpu.VMEM(spectra.shape[1:], kind),
+            pltpu.VMEM(spectra.shape[1:], kind),
             pltpu.SMEM(freq_idx.shape, freq_idx.dtype),
             pltpu.SMEM(pairing.shape, pairing.dtype),
             pltpu.VMEM((2, 2, 32, 2) + tile, kind),
             pltpu.VMEM((2, 32, 2, 2) + tile, kind),
             *[pltpu.VMEM((64, n) + tile, kind) for _ in range(4) for n in sizes],
             *[pltpu.VMEM((2, 16, n) + tile, kind) for _ in range(2) for n in sizes],
-            *[pltpu.VMEM((8 * rounds, n, 2) + tile, kind) for _ in range(4) for n in sizes],
-            pltpu.SemaphoreType.DMA((3,)),
+            *[
+                pltpu.VMEM(shape + tile, kind)
+                for _ in range(4)
+                for shape in ((16, rounds // 2, sizes[0], 2), (8 * rounds, sizes[1], 2))
+            ],
+            pltpu.SemaphoreType.DMA((4,)),
             pltpu.SemaphoreType.DMA((2, 4)),
             pltpu.SemaphoreType.DMA((2, 4)),
             pltpu.SemaphoreType.DMA((2, 2)),
@@ -372,7 +395,7 @@
             pltpu.SemaphoreType.DMA,
             pltpu.SemaphoreType.DMA,
             pltpu.SemaphoreType.DMA((2, 4)),
-            pltpu.SemaphoreType.DMA((rounds // 2,)),
+            pltpu.SemaphoreType.DMA((rounds // 2 + 1,)),
         ],
         compiler_params=pltpu.CompilerParams(
             collective_id=0, has_side_effects=True, vmem_limit_bytes=40 << 20

time: 86.4 us -> 87 us (level)
  no operation moved by 1% of the time
where the time goes in v6:
time: 87 us; the launch traced here: 86.9 us
  Pallas kernels  86.9 us (100%)
    pallas_call x1, Pallas kernels, move(): pl.pallas_call(move_kernel, out_shape=(pltpu.VMEM((rounds // 2, 32, 2, 2,...  82.2 us
    pallas_call x1, Pallas kernels, finish(): pl.pallas_call(functools.partial(finish_kernel, scale), out_shape=jax.Sha...  4.68 us

profile of v6, /device:TPU:1, one launch (start us, length us, event | category | flops | bytes accessed | tf_op | source)
XLA Modules:
  0.0 86.9 jit_solution(5116496408088625301)
XLA Ops:
  0.0 82.2 %move.1 = (bf16[3,32,2,2,2,2,16,128]{7,6,5,4,3,2,1,0:T(8,128)(2,1)S(1)}, bf16[32,256,128]{2,1,0:T(8,128)(2,1)S(1)}, bf16[2,4,32,128,128]{4,3,2,1,0:T(8,128)(2,1)S(1)}) custom-call(bf16[2,256,2,16,128]{4,3,2,1,0:T(8,128)(2,1)} %bitcast.1, s32[64]{0:T(128)} %freq_in.1, s32[6,64]{1,0:T(8,128)} %pairing_in.1), custom_call_target="tpu_custom_call" | custom-call | tf_op jit(solution)/shard_map/move/pallas_call | solution.py:361
  82.2 4.7 %finish.1 = bf16[2,6,32,128,128]{4,3,2,1,0:T(8,128)(2,1)} custom-call(bf16[3,32,2,2,2,2,16,128]{7,6,5,4,3,2,1,0:T(8,128)(2,1)S(1)} %get-tuple-element.8.part, bf16[32,256,128]{2,1,0:T(8,128)(2,1)S(1)} %get-tuple-element.9.left, bf16[2,4,32,128,128]{4,3,2,1,0:T(8,128)(2,1)S(1)} %get-tuple-element.10.done), custom_call_target="tpu_custom_call" | custom-call | tf_op jit(solution)/shard_map/finish/pallas_call | solution.py:441
